TPU v7x, 256 devices: a whole 4x4x8 slice. The times are simulated.
256 devices in a mesh: lon: 16 (over y, x_hi, core), lat: 16 (over x_lo, z).
Axes of the slice: x: 4 (x_hi: 2, x_lo: 2; x = x_hi * 2 + x_lo), y: 4, z: 8, core: 2. Of those that a mesh axis runs over, the one named last changes fastest.
Arguments:
- inputs: bfloat16 [2, 96, 192, 512], P(None, 'lat', 'lon'), may hold values from -6 to 6
- cotangent: bfloat16 [2, 96, 192, 512], P(None, 'lat', 'lon'), may hold values from -6 to 6
- gains: float32 [2, 512], replicated, may hold values from 0.1 to 1.9
- w_qkv: bfloat16 [2, 512, 1536], replicated, may hold values from -2 to 2
- w_out: bfloat16 [2, 512, 512], replicated, may hold values from -0.25 to 0.25
Outputs:
- grad_inputs: bfloat16 [2, 96, 192, 512], P(None, 'lat', 'lon')
- grad_qkv: float32 [2, 512, 1536], P(None, 'lon')
- grad_out: float32 [2, 512, 512], P(None, 'lon')
- grad_gains: float32 [2, 512], replicated
All inputs are finite; a program needn't handle non-finite values.
Results may differ from a plain program's by a relative error of at most 0.03.
Values may be sent and summed in bfloat16 or wider, within the bound.
A program may use at most 64 MiB of HBM per device.

v0:
```python
import jax
import jax.numpy as jnp
from jax import lax
from jax.sharding import PartitionSpec as P

HEADS = 8
LEV = 2
WLAT = 6
WLON = 12


epsilon = 1e-05
masked = -1e30


def shifted_2(x, axis, by):
    count = lax.axis_size(axis)
    return lax.ppermute(x, axis, [(i, (i + by) % count) for i in range(count)])


def product(form, left, right):
    return jnp.einsum(form, left, right, preferred_element_type=jnp.float32)


def inner_rows(left, right):
    return lax.dot_general(
        left, right, (((0,), (0,)), ((), ())), preferred_element_type=jnp.float32
    )


def outer_cols(left, right):
    return lax.dot_general(
        left, right, (((1,), (1,)), ((), ())), preferred_element_type=jnp.float32
    )


def to_windows(field_grid):
    levels, lat_rows, lon_cols, feature = field_grid.shape
    field_grid = field_grid.reshape(levels, lat_rows // WLAT, WLAT, lon_cols // WLON, WLON, feature)
    field_grid = field_grid.transpose(1, 3, 0, 2, 4, 5)
    return field_grid.reshape(lat_rows // WLAT, lon_cols // WLON, levels * WLAT * WLON, feature)


def from_windows(blocks):
    win_rows, win_cols, win_size, feature = blocks.shape
    blocks = blocks.reshape(win_rows, win_cols, LEV, WLAT, WLON, feature)
    blocks = blocks.transpose(2, 0, 3, 1, 4, 5)
    return blocks.reshape(LEV, win_rows * WLAT, win_cols * WLON, feature)


def region_windows(row_ids):
    per_row = row_ids.reshape(-1, WLAT)
    spread_ids = jnp.broadcast_to(per_row[:, None, :, None], (per_row.shape[0], LEV, WLAT, WLON))
    return spread_ids.reshape(per_row.shape[0], LEV * WLAT * WLON)


def window_scores(projected, region):
    win_cols, win_size, triple = projected.shape
    head_size = triple // (3 * HEADS)
    split_heads = projected.reshape(win_cols, win_size, 3, HEADS, head_size)
    queries = split_heads[:, :, 0]
    keys_all = split_heads[:, :, 1]
    values_all = split_heads[:, :, 2]
    scale = head_size ** (-0.5)
    scores = product("nihe,njhe->nhij", queries, keys_all) * scale
    same_region = region[:, None] == region[None, :]
    scores = jnp.where(same_region, scores, masked)
    row_max = jnp.max(scores, axis=-1, keepdims=True)
    exponent = jnp.exp(scores - row_max)
    weights = exponent / jnp.sum(exponent, axis=-1, keepdims=True)
    return (weights, queries, keys_all, values_all, scale)


def attend_forward(pair):
    projected, region = pair
    weights, queries, keys_all, values_all, scale = window_scores(projected, region)
    mixed = product("nhij,njhe->nihe", weights.astype(jnp.bfloat16), values_all)
    return mixed.reshape(projected.shape[0], projected.shape[1], -1).astype(jnp.bfloat16)


def attend_backward(triple_in):
    projected, region, grad_mixed = triple_in
    weights, queries, keys_all, values_all, scale = window_scores(projected, region)
    rounded = weights.astype(jnp.bfloat16)
    grad_heads = grad_mixed.reshape(queries.shape)
    grad_weights = product("nihe,njhe->nhij", grad_heads, values_all)
    grad_values = product("nhij,nihe->njhe", rounded, grad_heads).astype(jnp.bfloat16)
    grad_scores = weights * (grad_weights - jnp.sum(grad_weights * weights, axis=-1, keepdims=True))
    grad_scores = grad_scores.astype(jnp.bfloat16)
    grad_queries = (product("nhij,njhe->nihe", grad_scores, keys_all) * scale).astype(jnp.bfloat16)
    grad_keys = (product("nhij,nihe->njhe", grad_scores, queries) * scale).astype(jnp.bfloat16)
    stacked = jnp.stack([grad_queries, grad_keys, grad_values], axis=2)
    return stacked.reshape(projected.shape)


def layer_forward(blocks, gain_row, w_qkv, region):
    feature = blocks.shape[-1]
    values32 = blocks.astype(jnp.float32)
    center = jnp.mean(values32, axis=-1, keepdims=True)
    spread = jnp.mean(jnp.square(values32 - center), axis=-1, keepdims=True)
    inverse = lax.rsqrt(spread + epsilon)
    standard = (values32 - center) * inverse
    normed = (standard * gain_row).astype(jnp.bfloat16)
    projected = jnp.dot(
        normed.reshape(-1, feature), w_qkv, preferred_element_type=jnp.float32
    ).astype(jnp.bfloat16)
    projected = projected.reshape(blocks.shape[:-1] + (3 * feature,))
    attended = lax.map(attend_forward, (projected, region))
    return (standard, inverse, normed, projected, attended)


def layer_output(blocks, attended, w_out):
    feature = blocks.shape[-1]
    branch = jnp.dot(attended.reshape(-1, feature), w_out, preferred_element_type=jnp.float32)
    return (blocks.astype(jnp.float32) + branch.reshape(blocks.shape)).astype(jnp.bfloat16)


def layer_backward(grad_y, saved, gain_row, w_qkv, w_out, region):
    standard, inverse, normed, projected, attended = saved
    feature = grad_y.shape[-1]
    grad_flat = grad_y.reshape(-1, feature)
    grad_wout = inner_rows(attended.reshape(-1, feature), grad_flat)
    grad_att = outer_cols(grad_flat, w_out).astype(jnp.bfloat16).reshape(attended.shape)
    grad_proj = lax.map(attend_backward, (projected, region, grad_att))
    proj_flat = grad_proj.reshape(-1, 3 * feature)
    grad_wqkv = inner_rows(normed.reshape(-1, feature), proj_flat)
    grad_normed = outer_cols(proj_flat, w_qkv).reshape(standard.shape)
    grad_gain = jnp.sum(grad_normed * standard, axis=(0, 1, 2))
    scaled = grad_normed * gain_row
    centered = scaled - jnp.mean(scaled, axis=-1, keepdims=True)
    centered = centered - standard * jnp.mean(scaled * standard, axis=-1, keepdims=True)
    grad_in = grad_y.astype(jnp.float32) + inverse * centered
    return (grad_in.astype(jnp.bfloat16), grad_wqkv, grad_wout, grad_gain)


def shards(inputs, cotangent, gains, w_qkv, w_out):
    half_lat = WLAT // 2
    half_lon = WLON // 2
    lat_rows = inputs.shape[1]
    blocks = to_windows(inputs)
    plain_region = jnp.zeros((lat_rows // WLAT, LEV * WLAT * WLON), jnp.int32)
    saved_first = layer_forward(blocks, gains[0], w_qkv[0], plain_region)
    middle = from_windows(layer_output(blocks, saved_first[4], w_out[0]))
    rows_in = shifted_2((middle[:, :half_lat], cotangent[:, :half_lat]), "lat", -1)
    lat_frame = jnp.concatenate([middle[:, half_lat:], rows_in[0]], axis=1)
    lat_grad = jnp.concatenate([cotangent[:, half_lat:], rows_in[1]], axis=1)
    cols_in = shifted_2((lat_frame[:, :, :half_lon], lat_grad[:, :, :half_lon]), "lon", -1)
    shifted = jnp.concatenate([lat_frame[:, :, half_lon:], cols_in[0]], axis=2)
    shifted_grad = jnp.concatenate([lat_grad[:, :, half_lon:], cols_in[1]], axis=2)
    is_last = lax.axis_index("lat") == lax.axis_size("lat") - 1
    row_index = jnp.arange(lat_rows)
    row_ids = jnp.where((row_index >= lat_rows - half_lat) & is_last, 1, 0).astype(jnp.int32)
    region = region_windows(row_ids)
    saved_second = layer_forward(to_windows(shifted), gains[1], w_qkv[1], region)
    grad_shifted, qkv_second, out_second, gain_second = layer_backward(
        to_windows(shifted_grad), saved_second, gains[1], w_qkv[1], w_out[1], region
    )
    grad_frame = from_windows(grad_shifted)
    cols_back = shifted_2(grad_frame[:, :, -half_lon:], "lon", 1)
    grad_lat = jnp.concatenate([cols_back, grad_frame[:, :, :-half_lon]], axis=2)
    rows_back = shifted_2(grad_lat[:, -half_lat:], "lat", 1)
    grad_middle = jnp.concatenate([rows_back, grad_lat[:, :-half_lat]], axis=1)
    grad_blocks, qkv_first, out_first, gain_first = layer_backward(
        to_windows(grad_middle), saved_first, gains[0], w_qkv[0], w_out[0], plain_region
    )
    grads_qkv = jnp.stack([qkv_first, qkv_second])
    grads_out = jnp.stack([out_first, out_second])
    row_share = (
        lax.psum_scatter(
            grads_qkv.astype(jnp.bfloat16), "lon", scatter_dimension=1, tiled=True
        ).astype(jnp.float32),
        lax.psum_scatter(
            grads_out.astype(jnp.bfloat16), "lon", scatter_dimension=1, tiled=True
        ).astype(jnp.float32),
    )
    summed = (
        lax.psum(row_share[0].astype(jnp.bfloat16), "lat").astype(jnp.float32),
        lax.psum(row_share[1].astype(jnp.bfloat16), "lat").astype(jnp.float32),
    )
    gain_total = lax.psum(jnp.stack([gain_first, gain_second]), ("lon", "lat"))
    return (from_windows(grad_blocks), summed[0], summed[1], gain_total)


def solution(mesh):
    in_specs = (P(None, "lat", "lon", None), P(None, "lat", "lon", None), P(), P(), P())
    out_specs = (P(None, "lat", "lon", None), P(None, "lon", None), P(None, "lon", None), P())
    return jax.shard_map(shards, mesh=mesh, in_specs=in_specs, out_specs=out_specs, check_vma=False)
```

profile of v0, /device:TPU:2, one launch (start us, length us, event | category | flops | bytes accessed | tf_op | source)
XLA Modules:
  0.0 370.3 jit_solution(8873427577500725401)
XLA Ops:
  7.2 1.0 fusion.56
  8.2 5.9 %collective-permute-start = (bf16[2,3,12,512]{3,0,2,1:T(2,128)(2,1)S(1)}, bf16[2,3,12,512]{3,0,2,1:T(2,128)(2,1)S(1)}, u32[]{:S(2)}, u32[]{:S(2)}) collective-permute-start(bf16[2,3,12,512]{3,0,2,1:T(2,128)(2,1)S(1)} %get-tuple-element.89), channel_id=1, source_target_pairs={{0,15},{1,0},{2,1},{3,2},{4,3},{5,4},{6,5},{7,6},{8,7},{9,8},{10,9... | collective-permute-start | bytes 221192 | tf_op jit(solution)/shard_map/ppermute | solution.py:18
  14.2 1.1 convert_reduce_fusion
  15.3 1.0 copy.112
  18.1 1.8 convolution_convert_fusion.3
  20.8 0.9 convolution_convert_fusion.9
  22.5 1.2 fusion.31
  23.8 1.1 collective-permute-start.2
  25.7 2.7 collective-permute-done.2
  28.5 3.0 collective-permute-start.3
  31.7 2.2 collective-permute-start.1
  34.0 1.8 collective-permute-done.1
  36.5 1.1 pad_maximum_fusion.5
  40.2 1.9 convolution_convert_fusion.2
  42.9 1.2 fusion.59
  44.1 1.7 convolution_convert_fusion.6
  47.5 1.1 copy-done.18
  49.8 1.6 fusion.3
  51.4 6.1 %collective-permute-done.4 = bf16[2,6,6,512]{3,2,1,0:T(8,128)(2,1)S(1)} collective-permute-done((bf16[2,6,6,512]{3,2,1,0:T(8,128)(2,1)S(1)}, bf16[2,6,6,512]{3,2,1,0:T(8,128)(2,1)S(1)}, u32[]{:S(2)}, u32[]{:S(2)}) %collective-permute-start.4) | collective-permute-done | bytes 73760 | tf_op jit(solution)/shard_map/ppermute | solution.py:18
  58.1 6.4 %collective-permute-done.5 = bf16[2,3,12,512]{3,2,1,0:T(8,128)(2,1)S(1)} collective-permute-done((bf16[2,3,12,512]{3,2,1,0:T(8,128)(2,1)S(1)}, bf16[2,3,12,512]{3,2,1,0:T(8,128)(2,1)S(1)}, u32[]{:S(2)}, u32[]{:S(2)}) %collective-permute-start.5) | collective-permute-done | bytes 73760 | tf_op jit(solution)/shard_map/ppermute | solution.py:18
  64.6 1.4 convolution_convert_fusion.10
  66.0 2.1 fusion.19
  68.9 2.1 pad_maximum_fusion.1
  71.1 1.8 multiply_reduce_fusion
  76.0 1.9 pad_maximum_fusion
  78.0 2.3 multiply_reduce_fusion.3
  80.3 57.0 %reduce-scatter.5.cloned.1.call-done = bf16[2,32,512]{2,1,0:T(8,128)(2,1)} async-done(((bf16[2,512,512]{2,1,0:T(8,128)(2,1)}), bf16[2,32,512]{2,1,0:T(8,128)(2,1)}) %reduce-scatter.5.cloned.1.call-update) | async-done | bytes 65552 | tf_op jit(solution)/shard_map/reduce_scatter | solution.py:172
  137.4 86.9 %reduce-scatter.3.cloned.1.call-done = bf16[2,32,1536]{2,1,0:T(8,128)(2,1)} async-done(((bf16[2,512,1536]{2,1,0:T(8,128)(2,1)}), bf16[2,32,1536]{2,1,0:T(8,128)(2,1)}) %reduce-scatter.3.cloned.1.call-update) | async-done | bytes 196624 | tf_op jit(solution)/shard_map/reduce_scatter | solution.py:169
  225.3 75.2 %psum.23 = f32[2,512]{1,0:T(2,128)} all-reduce(f32[2,512]{1,0:T(2,128)S(1)} %pad_maximum_fusion.8), channel_id=1, replica_groups=mesh['lon'=16,'lat'=16] {'lon','lat'}, use_global_device_ids=true, to_apply=%region_20.21 | all-reduce | flops 1024 | bytes 8192 | tf_op jit(solution)/shard_map/psum | solution.py:180
  300.5 60.1 %all-reduce.3.cloned.1.call-done = (bf16[2,32,1536]{2,1,0:T(8,128)(2,1)}, bf16[2,32,512]{2,1,0:T(8,128)(2,1)}) async-done(((bf16[2,32,1536]{2,1,0:T(8,128)(2,1)}, bf16[2,32,512]{2,1,0:T(8,128)(2,1)}), (bf16[2,32,1536]{2,1,0:T(8,128)(2,1)}, bf16[2,32,512]{2,1,0:T(8,128)(2,1)})) %all-reduce.3.cloned.1.call-update) | async-done | bytes 262160 | tf_op jit(solution)/shard_map/psum | solution.py:177
  360.5 1.5 convert_element_type.310
  362.0 1.7 convert_element_type.305
  (114 shorter events, 17.2 us)
Async XLA Ops:
  7.2 9.2 %copy-start.17 = (f32[2,512]{1,0:T(2,128)S(1)}, f32[2,512]{1,0:T(2,128)}, u32[]{:S(2)}) copy-start(f32[2,512]{1,0:T(2,128)} %param.7) | copy-start | bytes 12292
  7.2 130.2 %reduce-scatter.5.cloned.1.call-start = ((), (), s32[]{:S(2)}) async-start(), calls=%async_computation.3 | async-start | bytes 1114112 | tf_op jit(solution)/shard_map/reduce_scatter | solution.py:172
  8.2 23.2 %collective-permute-start = (bf16[2,3,12,512]{3,0,2,1:T(2,128)(2,1)S(1)}, bf16[2,3,12,512]{3,0,2,1:T(2,128)(2,1)S(1)}, u32[]{:S(2)}, u32[]{:S(2)}) collective-permute-start(bf16[2,3,12,512]{3,0,2,1:T(2,128)(2,1)S(1)} %get-tuple-element.89), channel_id=1, source_target_pairs={{0,15},{1,0},{2,1},{3,2},{4,3},{5,4},{6,5},{7,6},{8,7},{9,8},{10,9... | collective-permute-start | bytes 221192 | tf_op jit(solution)/shard_map/ppermute | solution.py:18
  15.3 1.8 copy-start.2
  17.4 0.7 copy-start.5
  20.7 1.0 copy-start.14
  20.7 7.7 %copy-start.3 = (f32[8,144,144]{1,2,0:T(8,128)}, f32[8,144,144]{1,2,0:T(8,128)S(1)}, u32[]{:S(2)}) copy-start(f32[8,144,144]{1,2,0:T(8,128)S(1)} %get-tuple-element.93) | copy-start | bytes 1990660
  20.8 1.7 copy-start.8
  23.8 4.7 %collective-permute-start.2 = (bf16[2,3,12,512]{3,2,1,0:T(8,128)(2,1)S(1)}, bf16[2,3,12,512]{3,2,1,0:T(8,128)(2,1)S(1)}, u32[]{:S(2)}, u32[]{:S(2)}) collective-permute-start(bf16[2,3,12,512]{3,2,1,0:T(8,128)(2,1)S(1)} %get-tuple-element.85), channel_id=1, source_target_pairs={{0,15},{1,0},{2,1},{3,2},{4,3},{5,4},{6,5},{7,6},{8,7},{9,8},{10,9... | collective-permute-start | bytes 221192 | tf_op jit(solution)/shard_map/ppermute | solution.py:18
  28.5 5.3 %collective-permute-start.3 = (bf16[2,6,6,512]{3,2,1,0:T(8,128)(2,1)S(1)}, bf16[2,6,6,512]{3,2,1,0:T(8,128)(2,1)S(1)}, u32[]{:S(2)}, u32[]{:S(2)}) collective-permute-start(bf16[2,6,6,512]{3,2,1,0:T(8,128)(2,1)S(1)} %get-tuple-element.83), channel_id=1, source_target_pairs={{0,240},{16,0},{32,16},{48,32},{64,48},{80,64},{96,80},{112,96},{1... | collective-permute-start | bytes 221192 | tf_op jit(solution)/shard_map/ppermute | solution.py:18
  31.7 4.2 %collective-permute-start.1 = (bf16[2,6,6,512]{3,0,2,1:T(2,128)(2,1)S(1)}, bf16[2,6,6,512]{3,0,2,1:T(2,128)(2,1)S(1)}, u32[]{:S(2)}, u32[]{:S(2)}) collective-permute-start(bf16[2,6,6,512]{3,0,2,1:T(2,128)(2,1)S(1)} %get-tuple-element.87), channel_id=1, source_target_pairs={{0,240},{16,0},{32,16},{48,32},{64,48},{80,64},{96,80},{112,96},{1... | collective-permute-start | bytes 221192 | tf_op jit(solution)/shard_map/ppermute | solution.py:18
  33.9 3.7 copy-start.9
  35.8 0.6 copy-start.12
  37.6 11.8 %copy-start = (bf16[144,512]{1,0:T(8,128)(2,1)}, bf16[144,512]{1,0:T(8,128)(2,1)S(1)}, u32[]{:S(2)}) copy-start(bf16[144,512]{1,0:T(8,128)(2,1)S(1)} %reshape_transpose_reshape.17) | copy-start | bytes 442372
  42.1 0.8 copy-start.13
  44.1 1.7 copy-start.10
  44.1 1.7 copy-start.16
  46.7 1.9 copy-start.18
  49.7 8.1 %copy-start.1 = (bf16[144,512]{1,0:T(8,128)(2,1)S(1)}, bf16[144,512]{1,0:T(8,128)(2,1)}, u32[]{:S(2)}) copy-start(bf16[144,512]{1,0:T(8,128)(2,1)} %copy-done) | copy-start | bytes 442372
  49.7 8.1 %copy-start.7 = (bf16[8,64,144]{2,1,0:T(8,128)(2,1)S(1)}, bf16[8,64,144]{2,1,0:T(8,128)(2,1)}, u32[]{:S(2)}) copy-start(bf16[8,64,144]{2,1,0:T(8,128)(2,1)} %convolution_convert_fusion.6) | copy-start | bytes 442372
  49.7 7.8 %collective-permute-start.4 = (bf16[2,6,6,512]{3,2,1,0:T(8,128)(2,1)S(1)}, bf16[2,6,6,512]{3,2,1,0:T(8,128)(2,1)S(1)}, u32[]{:S(2)}, u32[]{:S(2)}) collective-permute-start(bf16[2,6,6,512]{3,2,1,0:T(8,128)(2,1)S(1)} %get-tuple-element.80), channel_id=1, source_target_pairs={{0,16},{16,32},{32,48},{48,64},{64,80},{80,96},{96,112},{112,128},... | collective-permute-start | bytes 221192 | tf_op jit(solution)/shard_map/ppermute | solution.py:18
  57.5 7.0 %collective-permute-start.5 = (bf16[2,3,12,512]{3,2,1,0:T(8,128)(2,1)S(1)}, bf16[2,3,12,512]{3,2,1,0:T(8,128)(2,1)S(1)}, u32[]{:S(2)}, u32[]{:S(2)}) collective-permute-start(bf16[2,3,12,512]{3,2,1,0:T(8,128)(2,1)S(1)} %fusion.45), channel_id=1, source_target_pairs={{0,1},{1,2},{2,3},{3,4},{4,5},{5,6},{6,7},{7,8},{8,9},{9,10},{10,1... | collective-permute-start | bytes 221192 | tf_op jit(solution)/shard_map/ppermute | solution.py:18
  68.9 2.2 copy-start.15
  71.0 153.2 %reduce-scatter.3.cloned.1.call-start = ((), (), s32[]{:S(2)}) async-start(), calls=%async_computation.2 | async-start | bytes 3342336 | tf_op jit(solution)/shard_map/reduce_scatter | solution.py:169
  71.1 1.8 copy-start.4
  73.2 1.0 copy-start.11
  74.4 0.9 copy-start.6
  78.0 282.6 %all-reduce.3.cloned.1.call-start = ((), (), s32[]{:S(2)}) async-start(), calls=%async_computation.4 | async-start | bytes 524288 | tf_op jit(solution)/shard_map/psum | solution.py:177
Sparse Core Ops, SparseCore 0:
  71.2 66.1 reduce-scatter.4
  142.3 81.8 reduce-scatter.2
  227.1 133.3 all-reduce.2
where the time goes:
time: 372 us; the launch traced here: 370 us
  waiting for transfers between devices  221 us (59%)
  blocking collectives  75.2 us (20%)
  matrix products  22.6 us (6%)
  between operations  14.3 us (4%)
  other arithmetic  12.7 us (3%)
  starting transfers between devices  12.6 us (3%)
  local copies, waits for them, and re-layouts  11.8 us (3%)
    reduce_scatter x1, waiting for transfers between devices, shards(): lax.psum_scatter(grads_qkv.astype(jnp.bfloat16), 'lon', scatter_dimension...  86.9 us
    psum x1, blocking collectives, shards(): gain_total = lax.psum(jnp.stack([gain_first, gain_second]), ('lon', 'lat'))  75.2 us
    psum x1, waiting for transfers between devices, shards(): lax.psum(row_share[0].astype(jnp.bfloat16), 'lat').astype(jnp.float32)  60.1 us
    reduce_scatter x1, waiting for transfers between devices, shards(): lax.psum_scatter(grads_out.astype(jnp.bfloat16), 'lon', scatter_dimension...  57 us
    ppermute x6, waiting for transfers between devices, shifted_2(): return lax.ppermute(x, axis, [(i, (i + by) % count) for i in range(count)])  17 us
    ppermute x6, starting transfers between devices, shifted_2(): return lax.ppermute(x, axis, [(i, (i + by) % count) for i in range(count)])  12.5 us
  transfers between devices with their start and end apart: 9, of which 7 were waited for; matrix products, arithmetic and copies ran while one was open for 5% of the time, Pallas kernels for 0%

commit v1 on v0

v1 whole, which is shorter than its diff:
```python
import functools

import jax
import jax.numpy as jnp
import numpy as np
from jax import lax
from jax.experimental import pallas as pl
from jax.experimental.pallas import tpu as pltpu
from jax.sharding import PartitionSpec as P

MESH = pl.DeviceIdType.MESH
F32 = jnp.float32
BF16 = jnp.bfloat16

HEADS = 8
LEV = 2
WLAT = 6
WLON = 12
D = 512
EPS = 1e-05
MASKED = -1e30
TOK = LEV * WLAT * WLON
QUAD = TOK // 4
PADQ = 48
STACK = 4 * TOK


def dot(a, b):
    return lax.dot_general(a, b, (((1,), (0,)), ((), ())), preferred_element_type=F32)


def dot_nt(a, b):
    return lax.dot_general(a, b, (((1,), (1,)), ((), ())), preferred_element_type=F32)


def dot_tn(a, b):
    return lax.dot_general(a, b, (((0,), (0,)), ((), ())), preferred_element_type=F32)


def slab_pieces():
    for lev in range(LEV):
        for row in range(WLAT):
            half_r, r = divmod(row, WLAT // 2)
            starts = [
                (half_r * 2 + half_c) * QUAD + lev * (QUAD // 2) + r * (WLON // 2)
                for half_c in range(2)
            ]
            yield lev, row, starts


def kernel(
    n_lat,
    n_lon,
    x_ref,
    c_ref,
    gains_ref,
    wq_ref,
    wo_ref,
    gx_ref,
    gq_ref,
    go_ref,
    gg_ref,
    xs,
    gy,
    std,
    inv,
    proj,
    qm,
    gam,
    probs,
    probs16,
    att,
    tmp,
    scores,
    ds,
    gp,
    gy16,
    na_own,
    na_out,
    na_in,
    gp_in,
    gy_in,
    hs,
    hr,
    gsend,
    r1a,
    r1b,
    acca,
    accb,
    r2a,
    r2b,
    acc2,
    r3,
    fin,
    gain_c,
    gain_y,
    gain_x,
    gain_z,
    send_sem,
    recv_sem,
):
    a = lax.axis_index("lat")
    b = lax.axis_index("lon")
    n_z = n_lat // 2
    n_y = n_lon // 4
    xlo, z = a // n_z, a % n_z
    y, xhi, core = b // 4, (b // 2) % 2, b % 2
    x = xhi * 2 + xlo

    def at(lat, lon):
        return {"lat": lat, "lon": lon}

    def at_x(xx):
        return at((xx % 2) * n_z + z, y * 4 + (xx // 2) * 2 + core)

    def at_y(yy):
        return at(a, yy * 4 + xhi * 2 + core)

    def at_z(zz):
        return at(xlo * n_z + zz, b)

    up_a, dn_a = (a + 1) % n_lat, (a + n_lat - 1) % n_lat
    up_b, dn_b = (b + 1) % n_lon, (b + n_lon - 1) % n_lon
    partner = at(a, y * 4 + xhi * 2 + (1 - core))
    halo_down = [at(dn_a, dn_b), at(dn_a, b), at(a, dn_b)]
    halo_up = [at(up_a, up_b), at(up_a, b), at(a, up_b)]

    greet = halo_down + halo_up + [partner]
    greet += [at_y((y + k) % n_y) for k in range(1, n_y)]
    greet += [at_x((x + k) % 4) for k in range(1, 4)]
    greet += [at((a + k) % n_lat, b) for k in range(1, n_lat)]
    barrier = pltpu.get_barrier_semaphore()
    for device in greet:
        pl.semaphore_signal(barrier, inc=1, device_id=device, device_id_type=MESH)

    count = [0]
    pending = []

    def remote(src, dst, device):
        i = count[0]
        count[0] += 1
        copy = pltpu.make_async_remote_copy(
            src_ref=src,
            dst_ref=dst,
            send_sem=send_sem.at[i],
            recv_sem=recv_sem.at[i],
            device_id=device,
            device_id_type=MESH,
        )
        copy.start()
        pending.append(copy)
        return copy

    def expect(i, src, dst, device):
        return pltpu.make_async_remote_copy(
            src_ref=src,
            dst_ref=dst,
            send_sem=send_sem.at[i],
            recv_sem=recv_sem.at[i],
            device_id=device,
            device_id_type=MESH,
        )

    lane = lax.broadcasted_iota(jnp.int32, (1, 256), 1)
    head_mask = [((lane >= 64 * h) & (lane < 64 * h + 64)).astype(F32) for h in range(4)]
    mask16 = [m.astype(BF16) for m in head_mask]
    scaled16 = [(m * 0.125).astype(BF16) for m in head_mask]

    r_id = lax.broadcasted_iota(jnp.int32, (D, D), 0)
    c_id = lax.broadcasted_iota(jnp.int32, (D, D), 1)
    low = c_id & 255
    which = jnp.where(c_id < 256, core, 1 - core)
    pick = (r_id == ((low >> 5) * 64 + which * 32 + (low & 31))).astype(F32).astype(BF16)

    def select_heads(stacked_ref):
        out = stacked_ref[0:TOK, :] * head_mask[0]
        for h in range(1, 4):
            out = jnp.where(head_mask[h] > 0.5, stacked_ref[h * TOK : (h + 1) * TOK, :], out)
        return out

    def forward(l):
        u = xs[l]
        center = jnp.mean(u, axis=-1, keepdims=True)
        u = u - center
        spread = jnp.mean(u * u, axis=-1, keepdims=True)
        inverse = lax.rsqrt(spread + EPS)
        standard = u * inverse
        std[l] = standard
        inv[l] = inverse
        normed = (standard * gains_ref[l : l + 1, :]).astype(BF16)
        proj[l] = dot(normed, wq_ref[l]).astype(BF16)
        both = dot(normed, pick).astype(BF16)
        na_own[l, 0] = both[:, :256]
        na_out[l, 0] = both[:, 256:]
        for t in range(2):
            q = proj[l, :, 256 * t : 256 * t + 256]
            k = proj[l, :, D + 256 * t : D + 256 * t + 256]
            v = proj[l, :, 2 * D + 256 * t : 2 * D + 256 * t + 256]
            for h in range(4):
                qm[l, t, h * TOK : (h + 1) * TOK, :] = q * scaled16[h]
            scores[...] = dot_nt(qm[l, t], k)
            for h in range(4):
                rows = slice(h * TOK, (h + 1) * TOK)
                s = scores[rows, :]
                if l == 1:
                    s = jnp.where(same_region, s, MASKED)
                e = jnp.exp(s - jnp.max(s, axis=-1, keepdims=True))
                p = e * (1.0 / jnp.sum(e, axis=-1, keepdims=True))
                probs[l, t, rows, :] = p
                probs16[l, t, rows, :] = p.astype(BF16)
            tmp[...] = dot(probs16[l, t], v)
            att[l, :, 256 * t : 256 * t + 256] = select_heads(tmp).astype(BF16)
        both = dot(att[l], pick).astype(BF16)
        na_own[l, 1] = both[:, :256]
        na_out[l, 1] = both[:, 256:]

    def backward_attention(l, t):
        k = proj[l, :, D + 256 * t : D + 256 * t + 256]
        v = proj[l, :, 2 * D + 256 * t : 2 * D + 256 * t + 256]
        g = dot_nt(gy16[l], wo_ref[l, 256 * t : 256 * t + 256, :]).astype(BF16)
        for h in range(4):
            gam[h * TOK : (h + 1) * TOK, :] = g * mask16[h]
        scores[...] = dot_nt(gam[...], v)
        gp[l, :, 2 * D + 256 * t : 2 * D + 256 * t + 256] = dot_tn(probs16[l, t], gam[...]).astype(BF16)
        for h in range(4):
            rows = slice(h * TOK, (h + 1) * TOK)
            p = probs[l, t, rows, :]
            g_p = scores[rows, :]
            total = jnp.sum(g_p * p, axis=-1, keepdims=True)
            ds[rows, :] = (p * (g_p - total)).astype(BF16)
        gp[l, :, D + 256 * t : D + 256 * t + 256] = dot_tn(ds[...], qm[l, t]).astype(BF16)
        tmp[...] = dot(ds[...], k)
        gp[l, :, 256 * t : 256 * t + 256] = (select_heads(tmp) * 0.125).astype(BF16)

    def backward_input(l):
        grad_normed = dot_nt(gp[l], wq_ref[l])
        standard = std[l]
        gain_rows = jnp.sum(grad_normed * standard, axis=0, keepdims=True)
        for j in range(4):
            gain_c[pl.ds(core, 1), l * 4 + j : l * 4 + j + 1, :] = gain_rows[
                :, j * 128 : (j + 1) * 128
            ].reshape(1, 1, 128)
        scaled = grad_normed * gains_ref[l : l + 1, :]
        m1 = jnp.mean(scaled, axis=-1, keepdims=True)
        m2 = jnp.mean(scaled * standard, axis=-1, keepdims=True)
        return gy[l] + inv[l] * (scaled - m1 - standard * m2)

    def store_weight_grads(l, lo, hi, kind):
        src = 0 if kind == "qkv" else 12
        cols = slice((lo - src) * 128, (hi - src) * 128)
        mine, theirs = (gp, gp_in) if kind == "qkv" else (gy16, gy_in)
        i = 0 if kind == "qkv" else 1
        g = dot_tn(na_own[l, i], mine[l, :, cols]) + dot_tn(na_in[l, i], theirs[l, :, cols])
        for cb in range(lo, hi):
            part = g[:, (cb - lo) * 128 : (cb - lo + 1) * 128].astype(BF16)
            gsend[l, :, :, cb] = part.reshape(n_y, 2, 32, 128)

    def stage1(l):
        out = []
        for k in range(1, n_y):
            yy = (y + k) % n_y
            out.append(remote(gsend.at[l, yy, :, 0:8], r1a.at[l, k - 1], at_y(yy)))
        for k in range(1, 4):
            xx = (x + k) % 4
            out.append(
                remote(
                    gsend.at[l, :, xx // 2, pl.ds(8 + 4 * (xx % 2), 4)],
                    r1b.at[l, k - 1],
                    at_x(xx),
                )
            )
        return out

    def stage2(l, copies):
        out = []
        for c in copies[: n_y - 1]:
            c.wait_recv()
        for i in range(2):
            total = gsend[l, y, i, 0:8].astype(F32)
            for k in range(n_y - 1):
                total = total + r1a[l, k, i].astype(F32)
            acca[l, i] = total.astype(BF16)
        for k in range(1, 4):
            xx = (x + k) % 4
            out.append(
                remote(acca.at[l, xx // 2, pl.ds(4 * (xx % 2), 4)], r2a.at[l, k - 1], at_x(xx))
            )
        for c in copies[n_y - 1 :]:
            c.wait_recv()
        for i in range(n_y):
            total = gsend[l, i, xhi, pl.ds(8 + 4 * xlo, 4)].astype(F32)
            for k in range(3):
                total = total + r1b[l, k, i].astype(F32)
            accb[l, i] = total.astype(BF16)
        for k in range(1, n_y):
            yy = (y + k) % n_y
            out.append(remote(accb.at[l, yy], r2b.at[l, k - 1], at_y(yy)))
        return out

    def stage3(l, copies):
        out = []
        for c in copies:
            c.wait_recv()
        total = acca[l, xhi, pl.ds(4 * xlo, 4)].astype(F32)
        for k in range(3):
            total = total + r2a[l, k].astype(F32)
        acc2[l, 0] = total.reshape(4, 2, 16, 128).astype(BF16)
        total = accb[l, y].astype(F32)
        for k in range(n_y - 1):
            total = total + r2b[l, k].astype(F32)
        acc2[l, 1] = total.reshape(4, 2, 16, 128).astype(BF16)
        for k in range(1, n_z):
            zz = (z + k) % n_z
            out.append(remote(acc2.at[l, :, zz // 2, zz % 2], r3.at[l, k - 1], at_z(zz)))
        return out

    def stage4(l, copies):
        out = []
        for c in copies:
            c.wait_recv()
        for i in range(2):
            total = acc2[l, i, z // 2, z % 2].astype(F32)
            for k in range(n_z - 1):
                total = total + r3[l, k, i].astype(F32)
            fin[l, xlo, i, z // 2, z % 2] = total.astype(BF16)
        mine = fin.at[l, xlo, :, z // 2, z % 2]
        for k in range(1, n_lat):
            i = count[0]
            remote(mine, mine, at((a + k) % n_lat, b))
            s = (a + n_lat - k) % n_lat
            sz = s % n_z
            theirs = fin.at[l, s // n_z, :, sz // 2, sz % 2]
            out.append(expect(i, theirs, theirs, at(s, b)))
        return out

    def finish(l, copies):
        for c in copies:
            c.wait_recv()
        for lo in range(2):
            for i in range(2):
                for cg in range(4):
                    part = fin[l, lo, i, cg].reshape(32, 128).astype(F32)
                    cb = i * 8 + lo * 4 + cg
                    if cb < 12:
                        gq_ref[l, :, cb * 128 : (cb + 1) * 128] = part
                    else:
                        go_ref[l, :, (cb - 12) * 128 : (cb - 11) * 128] = part

    def halo_send(step, field_ref, devices):
        copies = []
        for q in range(3):
            hs[step, q] = field_ref[q * QUAD : q * QUAD + PADQ, :].astype(BF16)
            copies.append(remote(hs.at[step, q], hr.at[step, q], devices[q]))
        return copies

    def halo_take(step, copies, field_ref):
        for q in range(3):
            copies[q].wait_recv()
            field_ref[q * QUAD : (q + 1) * QUAD, :] = hr[step, q].astype(F32)[:QUAD]

    for lev, row, starts in slab_pieces():
        slab = x_ref[lev, row].astype(F32)
        cot = c_ref[lev, row].astype(F32)
        for half in range(2):
            piece = slice(half * 6, half * 6 + 6)
            xs[0, starts[half] : starts[half] + 6, :] = slab[piece]
            gy[1, starts[half] : starts[half] + 6, :] = cot[piece]
    if n_lat > 1:
        last = a == n_lat - 1
    i_id = lax.broadcasted_iota(jnp.int32, (TOK, TOK), 0)
    j_id = lax.broadcasted_iota(jnp.int32, (TOK, TOK), 1)
    cut = jnp.where(last, TOK // 2, TOK)
    same_region = ((i_id < cut) & (j_id < cut)) | ((i_id >= cut) & (j_id >= cut))

    forward(0)
    pl.semaphore_wait(barrier, len(greet))
    cot_copies = halo_send(0, gy.at[1], halo_down)
    middle = xs[0] + dot(att[0], wo_ref[0])
    xs[1] = middle.astype(BF16).astype(F32)
    mid_copies = halo_send(1, xs.at[1], halo_down)
    na_copies = [remote(na_out.at[0], na_in.at[0], partner)]

    halo_take(0, cot_copies, gy.at[1])
    gy16[1] = gy[1].astype(BF16)
    gy_copies = [remote(gy16.at[1], gy_in.at[1], partner)]
    halo_take(1, mid_copies, xs.at[1])
    forward(1)
    na_copies.append(remote(na_out.at[1], na_in.at[1], partner))
    backward_attention(1, 0)
    backward_attention(1, 1)
    xs[1] = backward_input(1).astype(BF16).astype(F32)
    back_copies = halo_send(2, xs.at[1], halo_up)
    gp_copies = [remote(gp.at[1], gp_in.at[1], partner)]
    na_copies[1].wait_recv()
    gy_copies[0].wait_recv()
    store_weight_grads(1, 12, 16, "out")
    gp_copies[0].wait_recv()
    store_weight_grads(1, 0, 12, "qkv")
    s1 = stage1(1)

    gy[0, 3 * QUAD :, :] = xs[1, 3 * QUAD :, :]
    halo_take(2, back_copies, gy.at[0])
    gy16[0] = gy[0].astype(BF16)
    gy_copies.append(remote(gy16.at[0], gy_in.at[0], partner))
    backward_attention(0, 0)
    backward_attention(0, 1)
    gp_copies.append(remote(gp.at[0], gp_in.at[0], partner))
    s2 = stage2(1, s1)
    na_copies[0].wait_recv()
    gy_copies[1].wait_recv()
    store_weight_grads(0, 12, 16, "out")
    gp_copies[1].wait_recv()
    store_weight_grads(0, 0, 12, "qkv")
    t1 = stage1(0)
    s3 = stage3(1, s2)
    out = backward_input(0)
    xs[0] = out
    for lev, row, starts in slab_pieces():
        slab = jnp.concatenate([xs[0, s : s + 6, :] for s in starts], axis=0)
        gx_ref[lev, row] = slab.astype(BF16)

    def gain_step(buf, slot, peers):
        copies = []
        for other, device in peers:
            i = count[0]
            remote(buf.at[slot], buf.at[slot], device)
            copies.append((i, device))
        return copies

    def gain_wait(buf, n, me, copies, sources):
        for (i, device), s in zip(copies, sources):
            expect(i, buf.at[s], buf.at[s], device).wait_recv()
        total = buf[0]
        for j in range(1, n):
            total = total + buf[j]
        return total

    gc = gain_step(gain_c, core, [(1 - core, partner)])
    s4 = stage4(1, s3)
    gain_y[y] = gain_wait(gain_c, 2, core, gc, [1 - core])
    gc = gain_step(gain_y, y, [((y + k) % n_y, at_y((y + k) % n_y)) for k in range(1, n_y)])
    t2 = stage2(0, t1)
    gain_x[x] = gain_wait(gain_y, n_y, y, gc, [(y + n_y - k) % n_y for k in range(1, n_y)])
    gc = gain_step(gain_x, x, [((x + k) % 4, at_x((x + k) % 4)) for k in range(1, 4)])
    finish(1, s4)
    t3 = stage3(0, t2)
    gain_z[z] = gain_wait(gain_x, 4, x, gc, [(x + 4 - k) % 4 for k in range(1, 4)])
    gc = gain_step(gain_z, z, [((z + k) % n_z, at_z((z + k) % n_z)) for k in range(1, n_z)])
    t4 = stage4(0, t3)
    total = gain_wait(gain_z, n_z, z, gc, [(z + n_z - k) % n_z for k in range(1, n_z)])
    for l in range(2):
        for j in range(4):
            gg_ref[l : l + 1, j * 128 : (j + 1) * 128] = total[l * 4 + j : l * 4 + j + 1, :]
    finish(0, t4)
    for copy in pending:
        copy.wait_send()


N_COPIES = 160


def shards(n_lat, n_lon, inputs, cotangent, gains, w_qkv, w_out):
    n_y, n_z = n_lon // 4, n_lat // 2
    vmem = pl.BlockSpec(memory_space=pltpu.VMEM)
    scratch = [
        pltpu.VMEM((2, TOK, D), F32),
        pltpu.VMEM((2, TOK, D), F32),
        pltpu.VMEM((2, TOK, D), F32),
        pltpu.VMEM((2, TOK, 1), F32),
        pltpu.VMEM((2, TOK, 3 * D), BF16),
        pltpu.VMEM((2, 2, STACK, 256), BF16),
        pltpu.VMEM((STACK, 256), BF16),
        pltpu.VMEM((2, 2, STACK, TOK), F32),
        pltpu.VMEM((2, 2, STACK, TOK), BF16),
        pltpu.VMEM((2, TOK, D), BF16),
        pltpu.VMEM((STACK, 256), F32),
        pltpu.VMEM((STACK, TOK), F32),
        pltpu.VMEM((STACK, TOK), BF16),
        pltpu.VMEM((2, TOK, 3 * D), BF16),
        pltpu.VMEM((2, TOK, D), BF16),
        pltpu.VMEM((2, 2, TOK, 256), BF16),
        pltpu.VMEM((2, 2, TOK, 256), BF16),
        pltpu.VMEM((2, 2, TOK, 256), BF16),
        pltpu.VMEM((2, TOK, 3 * D), BF16),
        pltpu.VMEM((2, TOK, D), BF16),
        pltpu.VMEM((3, 3, PADQ, D), BF16),
        pltpu.VMEM((3, 3, PADQ, D), BF16),
        pltpu.VMEM((2, n_y, 2, 16, 32, 128), BF16),
        pltpu.VMEM((2, n_y - 1, 2, 8, 32, 128), BF16),
        pltpu.VMEM((2, 3, n_y, 4, 32, 128), BF16),
        pltpu.VMEM((2, 2, 8, 32, 128), BF16),
        pltpu.VMEM((2, n_y, 4, 32, 128), BF16),
        pltpu.VMEM((2, 3, 4, 32, 128), BF16),
        pltpu.VMEM((2, n_y - 1, 4, 32, 128), BF16),
        pltpu.VMEM((2, 2, 4, 2, 16, 128), BF16),
        pltpu.VMEM((2, n_z - 1, 2, 16, 128), BF16),
        pltpu.VMEM((2, 2, 2, 4, 2, 16, 128), BF16),
        pltpu.VMEM((2, 8, 128), F32),
        pltpu.VMEM((n_y, 8, 128), F32),
        pltpu.VMEM((4, 8, 128), F32),
        pltpu.VMEM((n_z, 8, 128), F32),
        pltpu.SemaphoreType.DMA((N_COPIES,)),
        pltpu.SemaphoreType.DMA((N_COPIES,)),
    ]
    return pl.pallas_call(
        functools.partial(kernel, n_lat, n_lon),
        out_shape=(
            jax.ShapeDtypeStruct(inputs.shape, BF16),
            jax.ShapeDtypeStruct((2, D // n_lon, 3 * D), F32),
            jax.ShapeDtypeStruct((2, D // n_lon, D), F32),
            jax.ShapeDtypeStruct((2, D), F32),
        ),
        in_specs=[vmem] * 5,
        out_specs=(vmem,) * 4,
        scratch_shapes=scratch,
        compiler_params=pltpu.CompilerParams(
            collective_id=0, has_side_effects=True, vmem_limit_bytes=56 * 2**20
        ),
    )(inputs, cotangent, gains, w_qkv, w_out)


def solution(mesh):
    in_specs = (P(None, "lat", "lon", None), P(None, "lat", "lon", None), P(), P(), P())
    out_specs = (P(None, "lat", "lon", None), P(None, "lon", None), P(None, "lon", None), P())
    return jax.shard_map(
        functools.partial(shards, mesh.shape["lat"], mesh.shape["lon"]),
        mesh=mesh,
        in_specs=in_specs,
        out_specs=out_specs,
        check_vma=False,
    )
```

time: 372 us -> 75.5 us (0.20)
  waiting for transfers between devices: 221 us -> 0 us
  blocking collectives: 75.2 us -> 0 us
  Pallas kernels: 0 us -> 64.1 us
  matrix products: 22.6 us -> 0 us
  between operations: 14.3 us -> 0.64 us
  other arithmetic: 12.7 us -> 0 us
  starting transfers between devices: 12.6 us -> 0 us
    reduce_scatter x2 -> x0, waiting for transfers between devices: 144 us -> none  [the longest x1 86.9 us: shards(): lax.psum_scatter(grads_qkv.astype(jnp.bfloat16), 'lon', scatter_dimension...]
    psum x1 -> x0, blocking collectives: 75.2 us -> none  [shards(): gain_total = lax.psum(jnp.stack([gain_first, gain_second]), ('lon', 'lat'))]
    pallas_call x0 -> x1, Pallas kernels: none -> 64.1 us  [shards(): pl.pallas_call(functools.partial(kernel, n_lat, n_lon), out_shape=(jax.Sh...]
    psum x1 -> x0, waiting for transfers between devices: 60.1 us -> none  [shards(): lax.psum(row_share[0].astype(jnp.bfloat16), 'lat').astype(jnp.float32)]
    dot_general x21 -> x0, matrix products: 20.8 us -> none  [the longest x10 6.59 us: product(): return jnp.einsum(form, left, right, preferred_element_type=jnp.float32)]
    ppermute x6 -> x0, waiting for transfers between devices: 17 us -> none  [shifted_2(): return lax.ppermute(x, axis, [(i, (i + by) % count) for i in range(count)])]
    ppermute x6 -> x0, starting transfers between devices: 12.5 us -> none  [shifted_2(): return lax.ppermute(x, axis, [(i, (i + by) % count) for i in range(count)])]
    another operation x5 -> x0, other arithmetic: 4.45 us -> none  [the longest x1 2.13 us: shards(): grads_out = jnp.stack([out_first, out_second])]
  transfers between devices with their start and end apart: 9 -> 0, of which waited for: 7 -> 0; matrix products, arithmetic and copies ran while one was open for 5% -> 0% of each run, Pallas kernels for 0% -> 0%
where the time goes in v1:
time: 75.5 us; the launch traced here: 74.3 us
  Pallas kernels  64.1 us (85%)
  local copies, waits for them, and re-layouts  9.58 us (13%)
    pallas_call x1, Pallas kernels, shards(): pl.pallas_call(functools.partial(kernel, n_lat, n_lon), out_shape=(jax.Sh...  64.1 us
    unnamed x5, local copies, waits for them, and re-layouts  7.83 us
    pallas_call x1, local copies, waits for them, and re-layouts, shards(): pl.pallas_call(functools.partial(kernel, n_lat, n_lon), out_shape=(jax.Sh...  1.74 us

profile of v1, /device:TPU:2, one launch (start us, length us, event | category | flops | bytes accessed | tf_op | source)
XLA Modules:
  0.0 74.3 jit_solution(5305494027420230906)
XLA Ops:
  0.6 1.6 %copy.9.x_ref = bf16[2,6,12,512]{3,2,1,0:T(8,128)(2,1)} copy(bf16[2,6,12,512]{3,0,2,1:T(2,128)(2,1)} %param.5) | data formatting | bytes 294912 | tf_op args[0]
  2.2 1.6 %copy.10.c_ref = bf16[2,6,12,512]{3,2,1,0:T(8,128)(2,1)} copy(bf16[2,6,12,512]{3,0,2,1:T(2,128)(2,1)} %param.6) | data formatting | bytes 294912 | tf_op args[1]
  3.9 64.1 %shard_map.84 = (bf16[2,6,12,512]{3,2,1,0:T(8,128)(2,1)}, f32[2,32,1536]{2,1,0:T(8,128)}, f32[2,32,512]{2,1,0:T(8,128)}, f32[2,512]{1,0:T(2,128)}) custom-call(bf16[2,6,12,512]{3,2,1,0:T(8,128)(2,1)} %copy.9.x_ref, bf16[2,6,12,512]{3,2,1,0:T(8,128)(2,1)} %copy.10.c_ref, f32[2,512]{1,0:T(2,128)} %gains_ref.1, bf16[2,512,1536]{2,1,0:T(8,128)(2,1)} %wq_ref.1, ...), custom_call_target="tpu_custom_call" | custom-call | tf_op jit(solution)/shard_map/pallas_call | solution.py:505
  68.0 1.7 %copy.11 = bf16[2,6,12,512]{3,0,2,1:T(2,128)(2,1)} copy(bf16[2,6,12,512]{3,2,1,0:T(8,128)(2,1)} %get-tuple-element.4) | data formatting | bytes 294912 | tf_op jit(solution)/shard_map/pallas_call | solution.py:505
  69.7 1.8 %copy.15 = f32[2,32,1536]{2,1,0:T(8,128)} copy(f32[2,32,1536]{2,1,0:T(8,128)} %get-tuple-element.13) | data formatting | bytes 786432
  71.5 1.6 %copy.16 = f32[2,32,512]{2,1,0:T(8,128)} copy(f32[2,32,512]{2,1,0:T(8,128)} %get-tuple-element.14) | data formatting | bytes 262144
  73.0 1.3 %copy.17 = f32[2,512]{1,0:T(2,128)} copy(f32[2,512]{1,0:T(2,128)} %get-tuple-element.15) | data formatting | bytes 8192

commit v2 on v1

--- a/solution.py
+++ b/solution.py
@@ -38,14 +38,11 @@
 
 
 def slab_pieces():
-    for lev in range(LEV):
-        for row in range(WLAT):
-            half_r, r = divmod(row, WLAT // 2)
-            starts = [
-                (half_r * 2 + half_c) * QUAD + lev * (QUAD // 2) + r * (WLON // 2)
-                for half_c in range(2)
-            ]
-            yield lev, row, starts
+    for row in range(WLAT):
+        half_r, r = divmod(row, WLAT // 2)
+        for half_c in range(2):
+            start = (half_r * 2 + half_c) * QUAD + r * WLON
+            yield row, half_c * (WLON // 2), start
 
 
 def kernel(
@@ -57,8 +54,7 @@
     wq_ref,
     wo_ref,
     gx_ref,
-    gq_ref,
-    go_ref,
+    fin_ref,
     gg_ref,
     xs,
     gy,
@@ -214,14 +210,17 @@
         na_own[l, 1] = both[:, :256]
         na_out[l, 1] = both[:, 256:]
 
-    def backward_attention(l, t):
+    def backward_values(l, t):
+        cols = slice(256 * t, 256 * t + 256)
+        g = dot_nt(gy16[l], wo_ref[l, cols, :]).astype(BF16)
+        for h in range(4):
+            gam[t, h * TOK : (h + 1) * TOK, :] = g * mask16[h]
+        gp[l, :, 2 * D + 256 * t : 2 * D + 256 * t + 256] = dot_tn(probs16[l, t], gam[t]).astype(BF16)
+
+    def backward_scores(l, t):
         k = proj[l, :, D + 256 * t : D + 256 * t + 256]
         v = proj[l, :, 2 * D + 256 * t : 2 * D + 256 * t + 256]
-        g = dot_nt(gy16[l], wo_ref[l, 256 * t : 256 * t + 256, :]).astype(BF16)
-        for h in range(4):
-            gam[h * TOK : (h + 1) * TOK, :] = g * mask16[h]
-        scores[...] = dot_nt(gam[...], v)
-        gp[l, :, 2 * D + 256 * t : 2 * D + 256 * t + 256] = dot_tn(probs16[l, t], gam[...]).astype(BF16)
+        scores[...] = dot_nt(gam[t], v)
         for h in range(4):
             rows = slice(h * TOK, (h + 1) * TOK)
             p = probs[l, t, rows, :]
@@ -245,70 +244,76 @@
         m2 = jnp.mean(scaled * standard, axis=-1, keepdims=True)
         return gy[l] + inv[l] * (scaled - m1 - standard * m2)
 
-    def store_weight_grads(l, lo, hi, kind):
-        src = 0 if kind == "qkv" else 12
-        cols = slice((lo - src) * 128, (hi - src) * 128)
-        mine, theirs = (gp, gp_in) if kind == "qkv" else (gy16, gy_in)
-        i = 0 if kind == "qkv" else 1
-        g = dot_tn(na_own[l, i], mine[l, :, cols]) + dot_tn(na_in[l, i], theirs[l, :, cols])
-        for cb in range(lo, hi):
-            part = g[:, (cb - lo) * 128 : (cb - lo + 1) * 128].astype(BF16)
-            gsend[l, :, :, cb] = part.reshape(n_y, 2, 32, 128)
-
-    def stage1(l):
+    def send_gp(l, cols):
+        return remote(gp.at[l, :, cols], gp_in.at[l, :, cols], partner)
+
+    def weight_grad(l, c, first, i, mine, theirs):
+        g = dot_tn(na_own[l, i], mine) + dot_tn(na_in[l, i], theirs)
+        for j in range(4):
+            part = g[:, j * 128 : (j + 1) * 128].astype(BF16)
+            gsend[l, c, :, :, first + j] = part.reshape(n_y, 2, 32, 128)
+
+    def value_out_grads(l):
+        weight_grad(l, 0, 4, 1, gy16[l], gy_in[l])
+        weight_grad(l, 0, 0, 0, gp[l, :, 2 * D :], gp_in[l, :, 2 * D :])
+
+    def query_key_grads(l):
+        weight_grad(l, 1, 0, 0, gp[l, :, :D], gp_in[l, :, :D])
+        weight_grad(l, 1, 4, 0, gp[l, :, D : 2 * D], gp_in[l, :, D : 2 * D])
+
+    def stage1(l, c):
         out = []
-        for k in range(1, n_y):
-            yy = (y + k) % n_y
-            out.append(remote(gsend.at[l, yy, :, 0:8], r1a.at[l, k - 1], at_y(yy)))
         for k in range(1, 4):
+            if k < n_y:
+                yy = (y + k) % n_y
+                out.append(remote(gsend.at[l, c, yy, :, 0:4], r1a.at[l, c, k - 1], at_y(yy)))
             xx = (x + k) % 4
             out.append(
                 remote(
-                    gsend.at[l, :, xx // 2, pl.ds(8 + 4 * (xx % 2), 4)],
-                    r1b.at[l, k - 1],
+                    gsend.at[l, c, :, xx // 2, pl.ds(4 + 2 * (xx % 2), 2)],
+                    r1b.at[l, c, k - 1],
                     at_x(xx),
                 )
             )
         return out
 
-    def stage2(l, copies):
+    def stage2(l, c, copies):
         out = []
-        for c in copies[: n_y - 1]:
-            c.wait_recv()
+        for copy in copies:
+            copy.wait_recv()
         for i in range(2):
-            total = gsend[l, y, i, 0:8].astype(F32)
+            total = gsend[l, c, y, i, 0:4].astype(F32)
             for k in range(n_y - 1):
-                total = total + r1a[l, k, i].astype(F32)
-            acca[l, i] = total.astype(BF16)
+                total = total + r1a[l, c, k, i].astype(F32)
+            acca[l, c, i] = total.astype(BF16)
         for k in range(1, 4):
             xx = (x + k) % 4
-            out.append(
-                remote(acca.at[l, xx // 2, pl.ds(4 * (xx % 2), 4)], r2a.at[l, k - 1], at_x(xx))
-            )
-        for c in copies[n_y - 1 :]:
-            c.wait_recv()
+            src = acca.at[l, c, xx // 2, pl.ds(2 * (xx % 2), 2)]
+            out.append(remote(src, r2a.at[l, c, k - 1], at_x(xx)))
         for i in range(n_y):
-            total = gsend[l, i, xhi, pl.ds(8 + 4 * xlo, 4)].astype(F32)
+            total = gsend[l, c, i, xhi, pl.ds(4 + 2 * xlo, 2)].astype(F32)
             for k in range(3):
-                total = total + r1b[l, k, i].astype(F32)
-            accb[l, i] = total.astype(BF16)
+                total = total + r1b[l, c, k, i].astype(F32)
+            accb[l, c, i] = total.astype(BF16)
         for k in range(1, n_y):
             yy = (y + k) % n_y
-            out.append(remote(accb.at[l, yy], r2b.at[l, k - 1], at_y(yy)))
+            out.append(remote(accb.at[l, c, yy], r2b.at[l, c, k - 1], at_y(yy)))
         return out
 
-    def stage3(l, copies):
+    def stage3_sum(l, c, copies):
+        for copy in copies:
+            copy.wait_recv()
+        total = acca[l, c, xhi, pl.ds(2 * xlo, 2)].astype(F32)
+        for k in range(3):
+            total = total + r2a[l, c, k].astype(F32)
+        acc2[l, c, 0:2] = total.reshape(2, 2, 16, 128).astype(BF16)
+        total = accb[l, c, y].astype(F32)
+        for k in range(n_y - 1):
+            total = total + r2b[l, c, k].astype(F32)
+        acc2[l, c, 2:4] = total.reshape(2, 2, 16, 128).astype(BF16)
+
+    def stage3(l):
         out = []
-        for c in copies:
-            c.wait_recv()
-        total = acca[l, xhi, pl.ds(4 * xlo, 4)].astype(F32)
-        for k in range(3):
-            total = total + r2a[l, k].astype(F32)
-        acc2[l, 0] = total.reshape(4, 2, 16, 128).astype(BF16)
-        total = accb[l, y].astype(F32)
-        for k in range(n_y - 1):
-            total = total + r2b[l, k].astype(F32)
-        acc2[l, 1] = total.reshape(4, 2, 16, 128).astype(BF16)
         for k in range(1, n_z):
             zz = (z + k) % n_z
             out.append(remote(acc2.at[l, :, zz // 2, zz % 2], r3.at[l, k - 1], at_z(zz)))
@@ -316,13 +321,12 @@
 
     def stage4(l, copies):
         out = []
-        for c in copies:
-            c.wait_recv()
-        for i in range(2):
-            total = acc2[l, i, z // 2, z % 2].astype(F32)
-            for k in range(n_z - 1):
-                total = total + r3[l, k, i].astype(F32)
-            fin[l, xlo, i, z // 2, z % 2] = total.astype(BF16)
+        for copy in copies:
+            copy.wait_recv()
+        total = acc2[l, :, z // 2, z % 2].astype(F32)
+        for k in range(n_z - 1):
+            total = total + r3[l, k].astype(F32)
+        fin[l, xlo, :, z // 2, z % 2] = total.astype(BF16)
         mine = fin.at[l, xlo, :, z // 2, z % 2]
         for k in range(1, n_lat):
             i = count[0]
@@ -334,17 +338,9 @@
         return out
 
     def finish(l, copies):
-        for c in copies:
-            c.wait_recv()
-        for lo in range(2):
-            for i in range(2):
-                for cg in range(4):
-                    part = fin[l, lo, i, cg].reshape(32, 128).astype(F32)
-                    cb = i * 8 + lo * 4 + cg
-                    if cb < 12:
-                        gq_ref[l, :, cb * 128 : (cb + 1) * 128] = part
-                    else:
-                        go_ref[l, :, (cb - 12) * 128 : (cb - 11) * 128] = part
+        for copy in copies:
+            copy.wait_recv()
+        fin_ref[l] = fin[l]
 
     def halo_send(step, field_ref, devices):
         copies = []
@@ -358,15 +354,11 @@
             copies[q].wait_recv()
             field_ref[q * QUAD : (q + 1) * QUAD, :] = hr[step, q].astype(F32)[:QUAD]
 
-    for lev, row, starts in slab_pieces():
-        slab = x_ref[lev, row].astype(F32)
-        cot = c_ref[lev, row].astype(F32)
-        for half in range(2):
-            piece = slice(half * 6, half * 6 + 6)
-            xs[0, starts[half] : starts[half] + 6, :] = slab[piece]
-            gy[1, starts[half] : starts[half] + 6, :] = cot[piece]
-    if n_lat > 1:
-        last = a == n_lat - 1
+    for row, col, start in slab_pieces():
+        cols = slice(col, col + WLON // 2)
+        xs[0, start : start + WLON, :] = x_ref[row, cols].astype(F32).reshape(WLON, D)
+        gy[1, start : start + WLON, :] = c_ref[row, cols].astype(F32).reshape(WLON, D)
+    last = a == n_lat - 1
     i_id = lax.broadcasted_iota(jnp.int32, (TOK, TOK), 0)
     j_id = lax.broadcasted_iota(jnp.int32, (TOK, TOK), 1)
     cut = jnp.where(last, TOK // 2, TOK)
@@ -386,38 +378,47 @@
     halo_take(1, mid_copies, xs.at[1])
     forward(1)
     na_copies.append(remote(na_out.at[1], na_in.at[1], partner))
-    backward_attention(1, 0)
-    backward_attention(1, 1)
+    backward_values(1, 0)
+    backward_values(1, 1)
+    v_copies = [send_gp(1, slice(2 * D, 3 * D))]
+    backward_scores(1, 0)
+    backward_scores(1, 1)
+    qk_copies = [send_gp(1, slice(0, 2 * D))]
     xs[1] = backward_input(1).astype(BF16).astype(F32)
     back_copies = halo_send(2, xs.at[1], halo_up)
-    gp_copies = [remote(gp.at[1], gp_in.at[1], partner)]
+    gy[0, 3 * QUAD :, :] = xs[1, 3 * QUAD :, :]
     na_copies[1].wait_recv()
     gy_copies[0].wait_recv()
-    store_weight_grads(1, 12, 16, "out")
-    gp_copies[0].wait_recv()
-    store_weight_grads(1, 0, 12, "qkv")
-    s1 = stage1(1)
-
-    gy[0, 3 * QUAD :, :] = xs[1, 3 * QUAD :, :]
+    v_copies[0].wait_recv()
+    value_out_grads(1)
+    s1v = stage1(1, 0)
+    qk_copies[0].wait_recv()
+    query_key_grads(1)
+    s1q = stage1(1, 1)
+
     halo_take(2, back_copies, gy.at[0])
     gy16[0] = gy[0].astype(BF16)
     gy_copies.append(remote(gy16.at[0], gy_in.at[0], partner))
-    backward_attention(0, 0)
-    backward_attention(0, 1)
-    gp_copies.append(remote(gp.at[0], gp_in.at[0], partner))
-    s2 = stage2(1, s1)
+    backward_values(0, 0)
+    backward_values(0, 1)
+    v_copies.append(send_gp(0, slice(2 * D, 3 * D)))
+    backward_scores(0, 0)
     na_copies[0].wait_recv()
     gy_copies[1].wait_recv()
-    store_weight_grads(0, 12, 16, "out")
-    gp_copies[1].wait_recv()
-    store_weight_grads(0, 0, 12, "qkv")
-    t1 = stage1(0)
-    s3 = stage3(1, s2)
-    out = backward_input(0)
-    xs[0] = out
-    for lev, row, starts in slab_pieces():
-        slab = jnp.concatenate([xs[0, s : s + 6, :] for s in starts], axis=0)
-        gx_ref[lev, row] = slab.astype(BF16)
+    v_copies[1].wait_recv()
+    value_out_grads(0)
+    t1v = stage1(0, 0)
+    backward_scores(0, 1)
+    qk_copies.append(send_gp(0, slice(0, 2 * D)))
+    s2v = stage2(1, 0, s1v)
+    qk_copies[1].wait_recv()
+    query_key_grads(0)
+    t1q = stage1(0, 1)
+    s2q = stage2(1, 1, s1q)
+    xs[0] = backward_input(0)
+    for row, col, start in slab_pieces():
+        piece = xs[0, start : start + WLON, :].reshape(WLON // 2, LEV, D)
+        gx_ref[row, col : col + WLON // 2] = piece.astype(BF16)
 
     def gain_step(buf, slot, peers):
         copies = []
@@ -436,27 +437,50 @@
         return total
 
     gc = gain_step(gain_c, core, [(1 - core, partner)])
-    s4 = stage4(1, s3)
+    t2v = stage2(0, 0, t1v)
+    stage3_sum(1, 0, s2v)
+    stage3_sum(1, 1, s2q)
+    s3 = stage3(1)
     gain_y[y] = gain_wait(gain_c, 2, core, gc, [1 - core])
     gc = gain_step(gain_y, y, [((y + k) % n_y, at_y((y + k) % n_y)) for k in range(1, n_y)])
-    t2 = stage2(0, t1)
+    t2q = stage2(0, 1, t1q)
     gain_x[x] = gain_wait(gain_y, n_y, y, gc, [(y + n_y - k) % n_y for k in range(1, n_y)])
     gc = gain_step(gain_x, x, [((x + k) % 4, at_x((x + k) % 4)) for k in range(1, 4)])
-    finish(1, s4)
-    t3 = stage3(0, t2)
+    stage3_sum(0, 0, t2v)
+    stage3_sum(0, 1, t2q)
+    t3 = stage3(0)
     gain_z[z] = gain_wait(gain_x, 4, x, gc, [(x + 4 - k) % 4 for k in range(1, 4)])
     gc = gain_step(gain_z, z, [((z + k) % n_z, at_z((z + k) % n_z)) for k in range(1, n_z)])
+    s4 = stage4(1, s3)
     t4 = stage4(0, t3)
     total = gain_wait(gain_z, n_z, z, gc, [(z + n_z - k) % n_z for k in range(1, n_z)])
     for l in range(2):
         for j in range(4):
             gg_ref[l : l + 1, j * 128 : (j + 1) * 128] = total[l * 4 + j : l * 4 + j + 1, :]
+    finish(1, s4)
     finish(0, t4)
     for copy in pending:
         copy.wait_send()
 
 
-N_COPIES = 160
+def unpack(gx_ref, fin_ref, gg_ref, gx_out, gq_out, go_out, gg_out):
+    gx_out[...] = gx_ref[...]
+    gg_out[...] = gg_ref[...]
+    for l in range(2):
+        for lo in range(2):
+            for j in range(2):
+                cols = slice((2 * lo + j) * 128, (2 * lo + j + 1) * 128)
+                block = [
+                    [fin_ref[l, lo, c, 2 * h + j].reshape(32, 128).astype(F32) for h in range(2)]
+                    for c in range(2)
+                ]
+                gq_out[l, :, cols] = block[1][0]
+                gq_out[l, :, D + cols.start : D + cols.stop] = block[1][1]
+                gq_out[l, :, 2 * D + cols.start : 2 * D + cols.stop] = block[0][0]
+                go_out[l, :, cols] = block[0][1]
+
+
+N_COPIES = 170
 
 
 def shards(n_lat, n_lon, inputs, cotangent, gains, w_qkv, w_out):
@@ -469,7 +493,7 @@
         pltpu.VMEM((2, TOK, 1), F32),
         pltpu.VMEM((2, TOK, 3 * D), BF16),
         pltpu.VMEM((2, 2, STACK, 256), BF16),
-        pltpu.VMEM((STACK, 256), BF16),
+        pltpu.VMEM((2, STACK, 256), BF16),
         pltpu.VMEM((2, 2, STACK, TOK), F32),
         pltpu.VMEM((2, 2, STACK, TOK), BF16),
         pltpu.VMEM((2, TOK, D), BF16),
@@ -485,13 +509,13 @@
         pltpu.VMEM((2, TOK, D), BF16),
         pltpu.VMEM((3, 3, PADQ, D), BF16),
         pltpu.VMEM((3, 3, PADQ, D), BF16),
-        pltpu.VMEM((2, n_y, 2, 16, 32, 128), BF16),
-        pltpu.VMEM((2, n_y - 1, 2, 8, 32, 128), BF16),
-        pltpu.VMEM((2, 3, n_y, 4, 32, 128), BF16),
-        pltpu.VMEM((2, 2, 8, 32, 128), BF16),
-        pltpu.VMEM((2, n_y, 4, 32, 128), BF16),
-        pltpu.VMEM((2, 3, 4, 32, 128), BF16),
-        pltpu.VMEM((2, n_y - 1, 4, 32, 128), BF16),
+        pltpu.VMEM((2, 2, n_y, 2, 8, 32, 128), BF16),
+        pltpu.VMEM((2, 2, n_y - 1, 2, 4, 32, 128), BF16),
+        pltpu.VMEM((2, 2, 3, n_y, 2, 32, 128), BF16),
+        pltpu.VMEM((2, 2, 2, 4, 32, 128), BF16),
+        pltpu.VMEM((2, 2, n_y, 2, 32, 128), BF16),
+        pltpu.VMEM((2, 2, 3, 2, 32, 128), BF16),
+        pltpu.VMEM((2, 2, n_y - 1, 2, 32, 128), BF16),
         pltpu.VMEM((2, 2, 4, 2, 16, 128), BF16),
         pltpu.VMEM((2, n_z - 1, 2, 16, 128), BF16),
         pltpu.VMEM((2, 2, 2, 4, 2, 16, 128), BF16),
@@ -502,21 +526,33 @@
         pltpu.SemaphoreType.DMA((N_COPIES,)),
         pltpu.SemaphoreType.DMA((N_COPIES,)),
     ]
-    return pl.pallas_call(
+    swap = (1, 2, 0, 3)
+    gx, fin, gg = pl.pallas_call(
         functools.partial(kernel, n_lat, n_lon),
         out_shape=(
-            jax.ShapeDtypeStruct(inputs.shape, BF16),
+            jax.ShapeDtypeStruct((WLAT, WLON, LEV, D), BF16),
+            jax.ShapeDtypeStruct((2, 2, 2, 4, 2, 16, 128), BF16),
+            jax.ShapeDtypeStruct((2, D), F32),
+        ),
+        in_specs=[vmem] * 5,
+        out_specs=(vmem,) * 3,
+        scratch_shapes=scratch,
+        compiler_params=pltpu.CompilerParams(
+            collective_id=0, has_side_effects=True, vmem_limit_bytes=56 * 2**20
+        ),
+    )(inputs.transpose(swap), cotangent.transpose(swap), gains, w_qkv, w_out)
+    gx, gq, go, gg = pl.pallas_call(
+        unpack,
+        out_shape=(
+            jax.ShapeDtypeStruct(gx.shape, BF16),
             jax.ShapeDtypeStruct((2, D // n_lon, 3 * D), F32),
             jax.ShapeDtypeStruct((2, D // n_lon, D), F32),
             jax.ShapeDtypeStruct((2, D), F32),
         ),
-        in_specs=[vmem] * 5,
+        in_specs=[vmem] * 3,
         out_specs=(vmem,) * 4,
-        scratch_shapes=scratch,
-        compiler_params=pltpu.CompilerParams(
-            collective_id=0, has_side_effects=True, vmem_limit_bytes=56 * 2**20
-        ),
-    )(inputs, cotangent, gains, w_qkv, w_out)
+    )(gx, fin, gg)
+    return gx.transpose(2, 0, 1, 3), gq, go, gg
 
 
 def solution(mesh):

time: 75.5 us -> 62.4 us (0.83); the launches traced: 74.3 us -> 62.3 us
  local copies, waits for them, and re-layouts: 9.58 us -> 0 us
  Pallas kernels: 64.1 us -> 61.6 us
    unnamed x5 -> x0, local copies, waits for them, and re-layouts: 7.83 us -> none
    pallas_call x1, Pallas kernels: 64.1 us -> 59.7 us  [shards(): pl.pallas_call(functools.partial(kernel, n_lat, n_lon), out_shape=(jax.Sh...]
    pallas_call x0 -> x1, Pallas kernels: none -> 1.88 us  [shards(): pl.pallas_call(unpack, out_shape=(jax.ShapeDtypeStruct(gx.shape, BF16), j...]
    pallas_call x1 -> x0, local copies, waits for them, and re-layouts: 1.74 us -> none  [shards(): pl.pallas_call(functools.partial(kernel, n_lat, n_lon), out_shape=(jax.Sh...]
where the time goes in v2:
time: 62.4 us; the launch traced here: 62.3 us
  Pallas kernels  61.6 us (99%)
  between operations  0.64 us (1%)
    pallas_call x1, Pallas kernels, shards(): pl.pallas_call(functools.partial(kernel, n_lat, n_lon), out_shape=(jax.Sh...  59.7 us
    pallas_call x1, Pallas kernels, shards(): pl.pallas_call(unpack, out_shape=(jax.ShapeDtypeStruct(gx.shape, BF16), j...  1.88 us

profile of v2, /device:TPU:2, one launch (start us, length us, event | category | flops | bytes accessed | tf_op | source)
XLA Modules:
  0.0 62.3 jit_solution(15994219491252553624)
XLA Ops:
  0.6 59.7 %shard_map.84 = (bf16[6,12,2,512]{3,2,1,0:T(2,128)(2,1)}, bf16[2,2,2,4,2,16,128]{6,5,4,3,2,1,0:T(8,128)(2,1)}, f32[2,512]{1,0:T(2,128)}) custom-call(bf16[6,12,2,512]{3,2,1,0:T(2,128)(2,1)} %bitcast.3, bf16[6,12,2,512]{3,2,1,0:T(2,128)(2,1)} %bitcast.4, f32[2,512]{1,0:T(2,128)} %gains_ref.1, bf16[2,512,1536]{2,1,0:T(8,128)(2,1)} %wq_ref.1, ...), custom_call_target="tpu_custom_call" | custom-call | tf_op jit(solution)/shard_map/pallas_call | solution.py:530
  60.4 1.9 %shard_map.85 = (bf16[6,12,2,512]{3,2,1,0:T(2,128)(2,1)}, f32[2,32,1536]{2,1,0:T(8,128)}, f32[2,32,512]{2,1,0:T(8,128)}, f32[2,512]{1,0:T(2,128)}) custom-call(bf16[6,12,2,512]{3,2,1,0:T(2,128)(2,1)} %get-tuple-element.11.gx_ref, bf16[2,2,2,4,2,16,128]{6,5,4,3,2,1,0:T(8,128)(2,1)} %get-tuple-element.12.fin_ref, f32[2,512]{1,0:T(2,128)} %get-tuple-element.13.gg_ref), custom_call_target="tpu_custom_call" | custom-call | tf_op jit(solution)/shard_map/pallas_call | solution.py:544

commit v3 on v2

--- a/solution.py
+++ b/solution.py
@@ -48,14 +48,20 @@
 def kernel(
     n_lat,
     n_lon,
+    x_hbm,
+    c_hbm,
+    gains_hbm,
+    wq_hbm,
+    wo_hbm,
+    gx_hbm,
+    fin_ref,
+    gg_ref,
     x_ref,
     c_ref,
     gains_ref,
     wq_ref,
     wo_ref,
     gx_ref,
-    fin_ref,
-    gg_ref,
     xs,
     gy,
     std,
@@ -87,13 +93,16 @@
     r2b,
     acc2,
     r3,
-    fin,
+    own4,
+    r4,
+    normed_ref,
     gain_c,
     gain_y,
     gain_x,
     gain_z,
     send_sem,
     recv_sem,
+    local_sem,
 ):
     a = lax.axis_index("lat")
     b = lax.axis_index("lon")
@@ -129,33 +138,43 @@
     for device in greet:
         pl.semaphore_signal(barrier, inc=1, device_id=device, device_id_type=MESH)
 
-    count = [0]
+    def local(i, src, dst):
+        copy = pltpu.make_async_copy(src, dst, local_sem.at[i])
+        copy.start()
+        return copy
+
+    loads = [
+        local(0, x_hbm, x_ref),
+        local(1, gains_hbm, gains_ref),
+        local(2, wq_hbm.at[0], wq_ref.at[0]),
+        local(3, wo_hbm.at[0], wo_ref.at[0]),
+        local(4, c_hbm, c_ref),
+        local(5, wq_hbm.at[1], wq_ref.at[1]),
+        local(6, wo_hbm.at[1], wo_ref.at[1]),
+    ]
+
     pending = []
 
-    def remote(src, dst, device):
-        i = count[0]
-        count[0] += 1
-        copy = pltpu.make_async_remote_copy(
-            src_ref=src,
-            dst_ref=dst,
-            send_sem=send_sem.at[i],
-            recv_sem=recv_sem.at[i],
-            device_id=device,
-            device_id_type=MESH,
-        )
-        copy.start()
-        pending.append(copy)
-        return copy
-
-    def expect(i, src, dst, device):
-        return pltpu.make_async_remote_copy(
-            src_ref=src,
-            dst_ref=dst,
-            send_sem=send_sem.at[i],
-            recv_sem=recv_sem.at[i],
-            device_id=device,
-            device_id_type=MESH,
-        )
+    def remote(whole, copies):
+        i = len(pending)
+
+        def describe(src, dst, device):
+            return pltpu.make_async_remote_copy(
+                src_ref=src,
+                dst_ref=dst,
+                send_sem=send_sem.at[i],
+                recv_sem=recv_sem.at[i],
+                device_id=device,
+                device_id_type=MESH,
+            )
+
+        for src, dst, device in copies:
+            describe(src, dst, device).start()
+        pending.append(describe(whole, whole, partner))
+        return pending[i]
+
+    def to_partner(src, dst):
+        return remote(dst, [(src, dst, partner)])
 
     lane = lax.broadcasted_iota(jnp.int32, (1, 256), 1)
     head_mask = [((lane >= 64 * h) & (lane < 64 * h + 64)).astype(F32) for h in range(4)]
@@ -184,10 +203,9 @@
         std[l] = standard
         inv[l] = inverse
         normed = (standard * gains_ref[l : l + 1, :]).astype(BF16)
+        loads[2 if l == 0 else 5].wait()
         proj[l] = dot(normed, wq_ref[l]).astype(BF16)
-        both = dot(normed, pick).astype(BF16)
-        na_own[l, 0] = both[:, :256]
-        na_out[l, 0] = both[:, 256:]
+        normed_ref[l] = normed
         for t in range(2):
             q = proj[l, :, 256 * t : 256 * t + 256]
             k = proj[l, :, D + 256 * t : D + 256 * t + 256]
@@ -206,9 +224,13 @@
                 probs16[l, t, rows, :] = p.astype(BF16)
             tmp[...] = dot(probs16[l, t], v)
             att[l, :, 256 * t : 256 * t + 256] = select_heads(tmp).astype(BF16)
-        both = dot(att[l], pick).astype(BF16)
-        na_own[l, 1] = both[:, :256]
-        na_out[l, 1] = both[:, 256:]
+
+    def share_rows(l):
+        for i, rows in enumerate((normed_ref, att)):
+            both = dot(rows[l], pick).astype(BF16)
+            na_own[l, i] = both[:, :256]
+            na_out[l, i] = both[:, 256:]
+        return to_partner(na_out.at[l], na_in.at[l])
 
     def backward_values(l, t):
         cols = slice(256 * t, 256 * t + 256)
@@ -236,16 +258,14 @@
         standard = std[l]
         gain_rows = jnp.sum(grad_normed * standard, axis=0, keepdims=True)
         for j in range(4):
-            gain_c[pl.ds(core, 1), l * 4 + j : l * 4 + j + 1, :] = gain_rows[
-                :, j * 128 : (j + 1) * 128
-            ].reshape(1, 1, 128)
+            gain_c[0, l * 4 + j : l * 4 + j + 1, :] = gain_rows[:, j * 128 : (j + 1) * 128]
         scaled = grad_normed * gains_ref[l : l + 1, :]
         m1 = jnp.mean(scaled, axis=-1, keepdims=True)
         m2 = jnp.mean(scaled * standard, axis=-1, keepdims=True)
         return gy[l] + inv[l] * (scaled - m1 - standard * m2)
 
     def send_gp(l, cols):
-        return remote(gp.at[l, :, cols], gp_in.at[l, :, cols], partner)
+        return to_partner(gp.at[l, :, cols], gp_in.at[l, :, cols])
 
     def weight_grad(l, c, first, i, mine, theirs):
         g = dot_tn(na_own[l, i], mine) + dot_tn(na_in[l, i], theirs)
@@ -262,43 +282,40 @@
         weight_grad(l, 1, 4, 0, gp[l, :, D : 2 * D], gp_in[l, :, D : 2 * D])
 
     def stage1(l, c):
-        out = []
+        over_y, over_x = [], []
         for k in range(1, 4):
             if k < n_y:
                 yy = (y + k) % n_y
-                out.append(remote(gsend.at[l, c, yy, :, 0:4], r1a.at[l, c, k - 1], at_y(yy)))
+                over_y.append((gsend.at[l, c, yy, :, 0:4], r1a.at[l, c, k - 1], at_y(yy)))
             xx = (x + k) % 4
-            out.append(
-                remote(
-                    gsend.at[l, c, :, xx // 2, pl.ds(4 + 2 * (xx % 2), 2)],
-                    r1b.at[l, c, k - 1],
-                    at_x(xx),
-                )
-            )
-        return out
+            src = gsend.at[l, c, :, xx // 2, pl.ds(4 + 2 * (xx % 2), 2)]
+            over_x.append((src, r1b.at[l, c, k - 1], at_x(xx)))
+        return remote(r1a.at[l, c], over_y), remote(r1b.at[l, c], over_x)
 
     def stage2(l, c, copies):
-        out = []
-        for copy in copies:
-            copy.wait_recv()
+        copies[0].wait_recv()
         for i in range(2):
             total = gsend[l, c, y, i, 0:4].astype(F32)
             for k in range(n_y - 1):
                 total = total + r1a[l, c, k, i].astype(F32)
             acca[l, c, i] = total.astype(BF16)
+        over_x = []
         for k in range(1, 4):
             xx = (x + k) % 4
             src = acca.at[l, c, xx // 2, pl.ds(2 * (xx % 2), 2)]
-            out.append(remote(src, r2a.at[l, c, k - 1], at_x(xx)))
+            over_x.append((src, r2a.at[l, c, k - 1], at_x(xx)))
+        over_x = remote(r2a.at[l, c], over_x)
+        copies[1].wait_recv()
         for i in range(n_y):
             total = gsend[l, c, i, xhi, pl.ds(4 + 2 * xlo, 2)].astype(F32)
             for k in range(3):
                 total = total + r1b[l, c, k, i].astype(F32)
             accb[l, c, i] = total.astype(BF16)
+        over_y = []
         for k in range(1, n_y):
             yy = (y + k) % n_y
-            out.append(remote(accb.at[l, c, yy], r2b.at[l, c, k - 1], at_y(yy)))
-        return out
+            over_y.append((accb.at[l, c, yy], r2b.at[l, c, k - 1], at_y(yy)))
+        return over_x, remote(r2b.at[l, c], over_y)
 
     def stage3_sum(l, c, copies):
         for copy in copies:
@@ -313,51 +330,48 @@
         acc2[l, c, 2:4] = total.reshape(2, 2, 16, 128).astype(BF16)
 
     def stage3(l):
-        out = []
+        over_z = []
         for k in range(1, n_z):
             zz = (z + k) % n_z
-            out.append(remote(acc2.at[l, :, zz // 2, zz % 2], r3.at[l, k - 1], at_z(zz)))
-        return out
+            over_z.append((acc2.at[l, :, zz // 2, zz % 2], r3.at[l, k - 1], at_z(zz)))
+        return remote(r3.at[l], over_z)
 
     def stage4(l, copies):
-        out = []
-        for copy in copies:
-            copy.wait_recv()
+        copies.wait_recv()
         total = acc2[l, :, z // 2, z % 2].astype(F32)
         for k in range(n_z - 1):
             total = total + r3[l, k].astype(F32)
-        fin[l, xlo, :, z // 2, z % 2] = total.astype(BF16)
-        mine = fin.at[l, xlo, :, z // 2, z % 2]
+        own4[l] = total.astype(BF16)
+        over_lat = []
         for k in range(1, n_lat):
-            i = count[0]
-            remote(mine, mine, at((a + k) % n_lat, b))
-            s = (a + n_lat - k) % n_lat
-            sz = s % n_z
-            theirs = fin.at[l, s // n_z, :, sz // 2, sz % 2]
-            out.append(expect(i, theirs, theirs, at(s, b)))
-        return out
+            over_lat.append((own4.at[l], r4.at[l, k - 1], at((a + k) % n_lat, b)))
+        return remote(r4.at[l], over_lat)
 
     def finish(l, copies):
-        for copy in copies:
-            copy.wait_recv()
-        fin_ref[l] = fin[l]
+        fin_ref[l, xlo, :, z // 2, z % 2] = own4[l]
+        copies.wait_recv()
+        for k in range(1, n_lat):
+            source = (a + n_lat - k) % n_lat
+            zz = source % n_z
+            fin_ref[l, source // n_z, :, zz // 2, zz % 2] = r4[l, k - 1]
 
     def halo_send(step, field_ref, devices):
         copies = []
         for q in range(3):
             hs[step, q] = field_ref[q * QUAD : q * QUAD + PADQ, :].astype(BF16)
-            copies.append(remote(hs.at[step, q], hr.at[step, q], devices[q]))
-        return copies
+            copies.append((hs.at[step, q], hr.at[step, q], devices[q]))
+        return remote(hr.at[step], copies)
 
     def halo_take(step, copies, field_ref):
+        copies.wait_recv()
         for q in range(3):
-            copies[q].wait_recv()
             field_ref[q * QUAD : (q + 1) * QUAD, :] = hr[step, q].astype(F32)[:QUAD]
 
+    loads[0].wait()
     for row, col, start in slab_pieces():
         cols = slice(col, col + WLON // 2)
         xs[0, start : start + WLON, :] = x_ref[row, cols].astype(F32).reshape(WLON, D)
-        gy[1, start : start + WLON, :] = c_ref[row, cols].astype(F32).reshape(WLON, D)
+    loads[1].wait()
     last = a == n_lat - 1
     i_id = lax.broadcasted_iota(jnp.int32, (TOK, TOK), 0)
     j_id = lax.broadcasted_iota(jnp.int32, (TOK, TOK), 1)
@@ -365,19 +379,24 @@
     same_region = ((i_id < cut) & (j_id < cut)) | ((i_id >= cut) & (j_id >= cut))
 
     forward(0)
-    pl.semaphore_wait(barrier, len(greet))
-    cot_copies = halo_send(0, gy.at[1], halo_down)
+    loads[3].wait()
     middle = xs[0] + dot(att[0], wo_ref[0])
     xs[1] = middle.astype(BF16).astype(F32)
+    pl.semaphore_wait(barrier, len(greet))
     mid_copies = halo_send(1, xs.at[1], halo_down)
-    na_copies = [remote(na_out.at[0], na_in.at[0], partner)]
-
+    loads[4].wait()
+    for row, col, start in slab_pieces():
+        cols = slice(col, col + WLON // 2)
+        gy[1, start : start + WLON, :] = c_ref[row, cols].astype(F32).reshape(WLON, D)
+    cot_copies = halo_send(0, gy.at[1], halo_down)
+    na_copies = [share_rows(0)]
+
+    halo_take(1, mid_copies, xs.at[1])
+    forward(1)
     halo_take(0, cot_copies, gy.at[1])
     gy16[1] = gy[1].astype(BF16)
-    gy_copies = [remote(gy16.at[1], gy_in.at[1], partner)]
-    halo_take(1, mid_copies, xs.at[1])
-    forward(1)
-    na_copies.append(remote(na_out.at[1], na_in.at[1], partner))
+    gy_copies = [to_partner(gy16.at[1], gy_in.at[1])]
+    loads[6].wait()
     backward_values(1, 0)
     backward_values(1, 1)
     v_copies = [send_gp(1, slice(2 * D, 3 * D))]
@@ -387,6 +406,7 @@
     xs[1] = backward_input(1).astype(BF16).astype(F32)
     back_copies = halo_send(2, xs.at[1], halo_up)
     gy[0, 3 * QUAD :, :] = xs[1, 3 * QUAD :, :]
+    na_copies.append(share_rows(1))
     na_copies[1].wait_recv()
     gy_copies[0].wait_recv()
     v_copies[0].wait_recv()
@@ -398,7 +418,7 @@
 
     halo_take(2, back_copies, gy.at[0])
     gy16[0] = gy[0].astype(BF16)
-    gy_copies.append(remote(gy16.at[0], gy_in.at[0], partner))
+    gy_copies.append(to_partner(gy16.at[0], gy_in.at[0]))
     backward_values(0, 0)
     backward_values(0, 1)
     v_copies.append(send_gp(0, slice(2 * D, 3 * D)))
@@ -419,46 +439,45 @@
     for row, col, start in slab_pieces():
         piece = xs[0, start : start + WLON, :].reshape(WLON // 2, LEV, D)
         gx_ref[row, col : col + WLON // 2] = piece.astype(BF16)
-
-    def gain_step(buf, slot, peers):
-        copies = []
-        for other, device in peers:
-            i = count[0]
-            remote(buf.at[slot], buf.at[slot], device)
-            copies.append((i, device))
-        return copies
-
-    def gain_wait(buf, n, me, copies, sources):
-        for (i, device), s in zip(copies, sources):
-            expect(i, buf.at[s], buf.at[s], device).wait_recv()
-        total = buf[0]
+    stores = [local(7, gx_ref, gx_hbm)]
+
+    def gain_send(buf, peers):
+        return remote(
+            buf.at[pl.ds(1, len(peers))],
+            [(buf.at[0], buf.at[k + 1], device) for k, device in enumerate(peers)],
+        )
+
+    def gain_sum(buf, copies, me, n):
+        copies.wait_recv()
+        total = buf[me]
         for j in range(1, n):
-            total = total + buf[j]
+            total = total + buf[(me + n - j) % n]
         return total
 
-    gc = gain_step(gain_c, core, [(1 - core, partner)])
+    g1 = gain_send(gain_c, [partner])
     t2v = stage2(0, 0, t1v)
     stage3_sum(1, 0, s2v)
     stage3_sum(1, 1, s2q)
     s3 = stage3(1)
-    gain_y[y] = gain_wait(gain_c, 2, core, gc, [1 - core])
-    gc = gain_step(gain_y, y, [((y + k) % n_y, at_y((y + k) % n_y)) for k in range(1, n_y)])
+    gain_y[0] = gain_sum(gain_c, g1, core, 2)
+    g2 = gain_send(gain_y, [at_y((y + k) % n_y) for k in range(1, n_y)])
     t2q = stage2(0, 1, t1q)
-    gain_x[x] = gain_wait(gain_y, n_y, y, gc, [(y + n_y - k) % n_y for k in range(1, n_y)])
-    gc = gain_step(gain_x, x, [((x + k) % 4, at_x((x + k) % 4)) for k in range(1, 4)])
+    gain_x[0] = gain_sum(gain_y, g2, y, n_y)
+    g3 = gain_send(gain_x, [at_x((x + k) % 4) for k in range(1, 4)])
     stage3_sum(0, 0, t2v)
     stage3_sum(0, 1, t2q)
     t3 = stage3(0)
-    gain_z[z] = gain_wait(gain_x, 4, x, gc, [(x + 4 - k) % 4 for k in range(1, 4)])
-    gc = gain_step(gain_z, z, [((z + k) % n_z, at_z((z + k) % n_z)) for k in range(1, n_z)])
+    gain_z[0] = gain_sum(gain_x, g3, x, 4)
+    g4 = gain_send(gain_z, [at_z((z + k) % n_z) for k in range(1, n_z)])
     s4 = stage4(1, s3)
     t4 = stage4(0, t3)
-    total = gain_wait(gain_z, n_z, z, gc, [(z + n_z - k) % n_z for k in range(1, n_z)])
+    total = gain_sum(gain_z, g4, z, n_z)
     for l in range(2):
         for j in range(4):
             gg_ref[l : l + 1, j * 128 : (j + 1) * 128] = total[l * 4 + j : l * 4 + j + 1, :]
     finish(1, s4)
     finish(0, t4)
+    stores[0].wait()
     for copy in pending:
         copy.wait_send()
 
@@ -480,13 +499,20 @@
                 go_out[l, :, cols] = block[0][1]
 
 
-N_COPIES = 170
+N_GROUPS = 35
 
 
 def shards(n_lat, n_lon, inputs, cotangent, gains, w_qkv, w_out):
     n_y, n_z = n_lon // 4, n_lat // 2
     vmem = pl.BlockSpec(memory_space=pltpu.VMEM)
+    hbm = pl.BlockSpec(memory_space=pl.ANY)
     scratch = [
+        pltpu.VMEM((WLAT, WLON, LEV, D), BF16),
+        pltpu.VMEM((WLAT, WLON, LEV, D), BF16),
+        pltpu.VMEM((2, D), F32),
+        pltpu.VMEM((2, D, 3 * D), BF16),
+        pltpu.VMEM((2, D, D), BF16),
+        pltpu.VMEM((WLAT, WLON, LEV, D), BF16),
         pltpu.VMEM((2, TOK, D), F32),
         pltpu.VMEM((2, TOK, D), F32),
         pltpu.VMEM((2, TOK, D), F32),
@@ -518,13 +544,16 @@
         pltpu.VMEM((2, 2, n_y - 1, 2, 32, 128), BF16),
         pltpu.VMEM((2, 2, 4, 2, 16, 128), BF16),
         pltpu.VMEM((2, n_z - 1, 2, 16, 128), BF16),
-        pltpu.VMEM((2, 2, 2, 4, 2, 16, 128), BF16),
+        pltpu.VMEM((2, 2, 16, 128), BF16),
+        pltpu.VMEM((2, n_lat - 1, 2, 16, 128), BF16),
+        pltpu.VMEM((2, TOK, D), BF16),
         pltpu.VMEM((2, 8, 128), F32),
         pltpu.VMEM((n_y, 8, 128), F32),
         pltpu.VMEM((4, 8, 128), F32),
         pltpu.VMEM((n_z, 8, 128), F32),
-        pltpu.SemaphoreType.DMA((N_COPIES,)),
-        pltpu.SemaphoreType.DMA((N_COPIES,)),
+        pltpu.SemaphoreType.DMA((N_GROUPS,)),
+        pltpu.SemaphoreType.DMA((N_GROUPS,)),
+        pltpu.SemaphoreType.DMA((8,)),
     ]
     swap = (1, 2, 0, 3)
     gx, fin, gg = pl.pallas_call(
@@ -534,8 +563,8 @@
             jax.ShapeDtypeStruct((2, 2, 2, 4, 2, 16, 128), BF16),
             jax.ShapeDtypeStruct((2, D), F32),
         ),
-        in_specs=[vmem] * 5,
-        out_specs=(vmem,) * 3,
+        in_specs=[hbm] * 5,
+        out_specs=(hbm, vmem, vmem),
         scratch_shapes=scratch,
         compiler_params=pltpu.CompilerParams(
             collective_id=0, has_side_effects=True, vmem_limit_bytes=56 * 2**20

time: 62.4 us -> 56.3 us (0.902)
  Pallas kernels: 61.6 us -> 55.6 us
    pallas_call x1, Pallas kernels: 59.7 us -> 53.7 us  [shards(): pl.pallas_call(functools.partial(kernel, n_lat, n_lon), out_shape=(jax.Sh...]
where the time goes in v3:
time: 56.3 us; the launch traced here: 56.2 us
  Pallas kernels  55.6 us (99%)
  between operations  0.64 us (1%)
    pallas_call x1, Pallas kernels, shards(): pl.pallas_call(functools.partial(kernel, n_lat, n_lon), out_shape=(jax.Sh...  53.7 us
    pallas_call x1, Pallas kernels, shards(): pl.pallas_call(unpack, out_shape=(jax.ShapeDtypeStruct(gx.shape, BF16), j...  1.88 us

profile of v3, /device:TPU:2, one launch (start us, length us, event | category | flops | bytes accessed | tf_op | source)
XLA Modules:
  0.0 56.2 jit_solution(13211171448508568178)
XLA Ops:
  0.6 53.7 %shard_map.84 = (bf16[6,12,2,512]{3,2,1,0:T(2,128)(2,1)}, bf16[2,2,2,4,2,16,128]{6,5,4,3,2,1,0:T(8,128)(2,1)}, f32[2,512]{1,0:T(2,128)}) custom-call(bf16[6,12,2,512]{3,2,1,0:T(2,128)(2,1)} %bitcast.3, bf16[6,12,2,512]{3,2,1,0:T(2,128)(2,1)} %bitcast.4, f32[2,512]{1,0:T(2,128)} %gains_hbm.1, bf16[2,512,1536]{2,1,0:T(8,128)(2,1)} %wq_hbm.1, ...), custom_call_target="tpu_custom_call" | custom-call | tf_op jit(solution)/shard_map/pallas_call | solution.py:559
  54.4 1.9 %shard_map.85 = (bf16[6,12,2,512]{3,2,1,0:T(2,128)(2,1)}, f32[2,32,1536]{2,1,0:T(8,128)}, f32[2,32,512]{2,1,0:T(8,128)}, f32[2,512]{1,0:T(2,128)}) custom-call(bf16[6,12,2,512]{3,2,1,0:T(2,128)(2,1)} %get-tuple-element.11.gx_ref, bf16[2,2,2,4,2,16,128]{6,5,4,3,2,1,0:T(8,128)(2,1)} %get-tuple-element.12.fin_ref, f32[2,512]{1,0:T(2,128)} %get-tuple-element.13.gg_ref), custom_call_target="tpu_custom_call" | custom-call | tf_op jit(solution)/shard_map/pallas_call | solution.py:573

commit v4 on v3

--- a/solution.py
+++ b/solution.py
@@ -35,6 +35,10 @@
 
 def dot_tn(a, b):
     return lax.dot_general(a, b, (((0,), (0,)), ((), ())), preferred_element_type=F32)
+
+
+def far_first(n):
+    return sorted(range(1, n), key=lambda k: -min(k, n - k))
 
 
 def slab_pieces():
@@ -96,6 +100,7 @@
     own4,
     r4,
     normed_ref,
+    part_g,
     gain_c,
     gain_y,
     gain_x,
@@ -133,7 +138,7 @@
     greet = halo_down + halo_up + [partner]
     greet += [at_y((y + k) % n_y) for k in range(1, n_y)]
     greet += [at_x((x + k) % 4) for k in range(1, 4)]
-    greet += [at((a + k) % n_lat, b) for k in range(1, n_lat)]
+    greet = [at((a + k) % n_lat, b) for k in far_first(n_lat)] + greet
     barrier = pltpu.get_barrier_semaphore()
     for device in greet:
         pl.semaphore_signal(barrier, inc=1, device_id=device, device_id_type=MESH)
@@ -277,13 +282,18 @@
         weight_grad(l, 0, 4, 1, gy16[l], gy_in[l])
         weight_grad(l, 0, 0, 0, gp[l, :, 2 * D :], gp_in[l, :, 2 * D :])
 
+    def query_key_own(l):
+        part_g[...] = dot_tn(na_own[l, 0], gp[l, :, : 2 * D])
+
     def query_key_grads(l):
-        weight_grad(l, 1, 0, 0, gp[l, :, :D], gp_in[l, :, :D])
-        weight_grad(l, 1, 4, 0, gp[l, :, D : 2 * D], gp_in[l, :, D : 2 * D])
+        g = part_g[...] + dot_tn(na_in[l, 0], gp_in[l, :, : 2 * D])
+        for j in range(8):
+            part = g[:, j * 128 : (j + 1) * 128].astype(BF16)
+            gsend[l, 1, :, :, j] = part.reshape(n_y, 2, 32, 128)
 
     def stage1(l, c):
         over_y, over_x = [], []
-        for k in range(1, 4):
+        for k in far_first(4):
             if k < n_y:
                 yy = (y + k) % n_y
                 over_y.append((gsend.at[l, c, yy, :, 0:4], r1a.at[l, c, k - 1], at_y(yy)))
@@ -300,7 +310,7 @@
                 total = total + r1a[l, c, k, i].astype(F32)
             acca[l, c, i] = total.astype(BF16)
         over_x = []
-        for k in range(1, 4):
+        for k in far_first(4):
             xx = (x + k) % 4
             src = acca.at[l, c, xx // 2, pl.ds(2 * (xx % 2), 2)]
             over_x.append((src, r2a.at[l, c, k - 1], at_x(xx)))
@@ -312,7 +322,7 @@
                 total = total + r1b[l, c, k, i].astype(F32)
             accb[l, c, i] = total.astype(BF16)
         over_y = []
-        for k in range(1, n_y):
+        for k in far_first(n_y):
             yy = (y + k) % n_y
             over_y.append((accb.at[l, c, yy], r2b.at[l, c, k - 1], at_y(yy)))
         return over_x, remote(r2b.at[l, c], over_y)
@@ -331,7 +341,7 @@
 
     def stage3(l):
         over_z = []
-        for k in range(1, n_z):
+        for k in far_first(n_z):
             zz = (z + k) % n_z
             over_z.append((acc2.at[l, :, zz // 2, zz % 2], r3.at[l, k - 1], at_z(zz)))
         return remote(r3.at[l], over_z)
@@ -343,7 +353,7 @@
             total = total + r3[l, k].astype(F32)
         own4[l] = total.astype(BF16)
         over_lat = []
-        for k in range(1, n_lat):
+        for k in sorted(range(1, n_lat), key=lambda k: -min(k % n_z, n_z - k % n_z)):
             over_lat.append((own4.at[l], r4.at[l, k - 1], at((a + k) % n_lat, b)))
         return remote(r4.at[l], over_lat)
 
@@ -412,6 +422,7 @@
     v_copies[0].wait_recv()
     value_out_grads(1)
     s1v = stage1(1, 0)
+    query_key_own(1)
     qk_copies[0].wait_recv()
     query_key_grads(1)
     s1q = stage1(1, 1)
@@ -431,6 +442,7 @@
     backward_scores(0, 1)
     qk_copies.append(send_gp(0, slice(0, 2 * D)))
     s2v = stage2(1, 0, s1v)
+    query_key_own(0)
     qk_copies[1].wait_recv()
     query_key_grads(0)
     t1q = stage1(0, 1)
@@ -467,9 +479,9 @@
     stage3_sum(0, 0, t2v)
     stage3_sum(0, 1, t2q)
     t3 = stage3(0)
+    s4 = stage4(1, s3)
     gain_z[0] = gain_sum(gain_x, g3, x, 4)
     g4 = gain_send(gain_z, [at_z((z + k) % n_z) for k in range(1, n_z)])
-    s4 = stage4(1, s3)
     t4 = stage4(0, t3)
     total = gain_sum(gain_z, g4, z, n_z)
     for l in range(2):
@@ -547,6 +559,7 @@
         pltpu.VMEM((2, 2, 16, 128), BF16),
         pltpu.VMEM((2, n_lat - 1, 2, 16, 128), BF16),
         pltpu.VMEM((2, TOK, D), BF16),
+        pltpu.VMEM((D // 2, 2 * D), F32),
         pltpu.VMEM((2, 8, 128), F32),
         pltpu.VMEM((n_y, 8, 128), F32),
         pltpu.VMEM((4, 8, 128), F32),

time: 56.3 us -> 54.8 us (0.973)
  Pallas kernels: 55.6 us -> 54.1 us
    pallas_call x1, Pallas kernels: 53.7 us -> 52.2 us  [shards(): pl.pallas_call(functools.partial(kernel, n_lat, n_lon), out_shape=(jax.Sh...]
where the time goes in v4:
time: 54.8 us; the launch traced here: 54.7 us
  Pallas kernels  54.1 us (99%)
  between operations  0.64 us (1%)
    pallas_call x1, Pallas kernels, shards(): pl.pallas_call(functools.partial(kernel, n_lat, n_lon), out_shape=(jax.Sh...  52.2 us
    pallas_call x1, Pallas kernels, shards(): pl.pallas_call(unpack, out_shape=(jax.ShapeDtypeStruct(gx.shape, BF16), j...  1.88 us

profile of v4, /device:TPU:2, one launch (start us, length us, event | category | flops | bytes accessed | tf_op | source)
XLA Modules:
  0.0 54.7 jit_solution(4443513477113154606)
XLA Ops:
  0.6 52.2 %shard_map.84 = (bf16[6,12,2,512]{3,2,1,0:T(2,128)(2,1)}, bf16[2,2,2,4,2,16,128]{6,5,4,3,2,1,0:T(8,128)(2,1)}, f32[2,512]{1,0:T(2,128)}) custom-call(bf16[6,12,2,512]{3,2,1,0:T(2,128)(2,1)} %bitcast.3, bf16[6,12,2,512]{3,2,1,0:T(2,128)(2,1)} %bitcast.4, f32[2,512]{1,0:T(2,128)} %gains_hbm.1, bf16[2,512,1536]{2,1,0:T(8,128)(2,1)} %wq_hbm.1, ...), custom_call_target="tpu_custom_call" | custom-call | tf_op jit(solution)/shard_map/pallas_call | solution.py:572
  52.9 1.9 %shard_map.85 = (bf16[6,12,2,512]{3,2,1,0:T(2,128)(2,1)}, f32[2,32,1536]{2,1,0:T(8,128)}, f32[2,32,512]{2,1,0:T(8,128)}, f32[2,512]{1,0:T(2,128)}) custom-call(bf16[6,12,2,512]{3,2,1,0:T(2,128)(2,1)} %get-tuple-element.11.gx_ref, bf16[2,2,2,4,2,16,128]{6,5,4,3,2,1,0:T(8,128)(2,1)} %get-tuple-element.12.fin_ref, f32[2,512]{1,0:T(2,128)} %get-tuple-element.13.gg_ref), custom_call_target="tpu_custom_call" | custom-call | tf_op jit(solution)/shard_map/pallas_call | solution.py:586

commit v5 on v4

--- a/solution.py
+++ b/solution.py
@@ -135,6 +135,14 @@
     halo_down = [at(dn_a, dn_b), at(dn_a, b), at(a, dn_b)]
     halo_up = [at(up_a, up_b), at(up_a, b), at(a, up_b)]
 
+    def local(i, src, dst):
+        copy = pltpu.make_async_copy(src, dst, local_sem.at[i])
+        copy.start()
+        return copy
+
+    loads = [local(0, x_hbm, x_ref), local(1, gains_hbm, gains_ref)]
+    loads.append(local(2, wq_hbm.at[0], wq_ref.at[0]))
+
     greet = halo_down + halo_up + [partner]
     greet += [at_y((y + k) % n_y) for k in range(1, n_y)]
     greet += [at_x((x + k) % 4) for k in range(1, 4)]
@@ -143,15 +151,7 @@
     for device in greet:
         pl.semaphore_signal(barrier, inc=1, device_id=device, device_id_type=MESH)
 
-    def local(i, src, dst):
-        copy = pltpu.make_async_copy(src, dst, local_sem.at[i])
-        copy.start()
-        return copy
-
-    loads = [
-        local(0, x_hbm, x_ref),
-        local(1, gains_hbm, gains_ref),
-        local(2, wq_hbm.at[0], wq_ref.at[0]),
+    loads += [
         local(3, wo_hbm.at[0], wo_ref.at[0]),
         local(4, c_hbm, c_ref),
         local(5, wq_hbm.at[1], wq_ref.at[1]),

time: 54.8 us -> 55 us (level)
  no operation moved by 1% of the time
where the time goes in v5:
time: 55 us; the launch traced here: 54.9 us
  Pallas kernels  54.3 us (99%)
  between operations  0.64 us (1%)
    pallas_call x1, Pallas kernels, shards(): pl.pallas_call(functools.partial(kernel, n_lat, n_lon), out_shape=(jax.Sh...  52.4 us
    pallas_call x1, Pallas kernels, shards(): pl.pallas_call(unpack, out_shape=(jax.ShapeDtypeStruct(gx.shape, BF16), j...  1.88 us

profile of v5, /device:TPU:2, one launch (start us, length us, event | category | flops | bytes accessed | tf_op | source)
XLA Modules:
  0.0 54.9 jit_solution(16888710052567379842)
XLA Ops:
  0.6 52.4 %shard_map.84 = (bf16[6,12,2,512]{3,2,1,0:T(2,128)(2,1)}, bf16[2,2,2,4,2,16,128]{6,5,4,3,2,1,0:T(8,128)(2,1)}, f32[2,512]{1,0:T(2,128)}) custom-call(bf16[6,12,2,512]{3,2,1,0:T(2,128)(2,1)} %bitcast.3, bf16[6,12,2,512]{3,2,1,0:T(2,128)(2,1)} %bitcast.4, f32[2,512]{1,0:T(2,128)} %gains_hbm.1, bf16[2,512,1536]{2,1,0:T(8,128)(2,1)} %wq_hbm.1, ...), custom_call_target="tpu_custom_call" | custom-call | tf_op jit(solution)/shard_map/pallas_call | solution.py:572
  53.0 1.9 %shard_map.85 = (bf16[6,12,2,512]{3,2,1,0:T(2,128)(2,1)}, f32[2,32,1536]{2,1,0:T(8,128)}, f32[2,32,512]{2,1,0:T(8,128)}, f32[2,512]{1,0:T(2,128)}) custom-call(bf16[6,12,2,512]{3,2,1,0:T(2,128)(2,1)} %get-tuple-element.11.gx_ref, bf16[2,2,2,4,2,16,128]{6,5,4,3,2,1,0:T(8,128)(2,1)} %get-tuple-element.12.fin_ref, f32[2,512]{1,0:T(2,128)} %get-tuple-element.13.gg_ref), custom_call_target="tpu_custom_call" | custom-call | tf_op jit(solution)/shard_map/pallas_call | solution.py:586
